TPU v7x, 256 devices: a whole 4x4x8 slice. The times are simulated.
256 devices in a mesh: batch: 16 (over y_hi, z), seq: 16 (over x, y_lo, core).
Axes of the slice: x: 4, y: 4 (y_hi: 2, y_lo: 2; y = y_hi * 2 + y_lo), z: 8, core: 2. Of those that a mesh axis runs over, the one named last changes fastest.
Arguments:
- forward_embed: bfloat16 [98304, 1536], P(('batch', 'seq')), parts along dimension 0, may hold values from -6 to 6
- reverse_embed: bfloat16 [98304, 1536], P(('batch', 'seq')), parts along dimension 0, may hold values from -6 to 6
- conv_weight: bfloat16 [1, 3, 1536, 1536], P(None, None, 'seq'), may hold values from -0.09375 to 0.09375
- conv_bias: float32 [1, 1536], replicated, may hold values from -0.5 to 0.5
- head_weight: bfloat16 [1536, 1024], replicated, may hold values from -0.15625 to 0.15625
- head_bias: float32 [1024], replicated, may hold values from -1 to 1
Outputs:
- averaged: bfloat16 [98304, 1024], P(('batch', 'seq')), parts along dimension 0
There are 16 independent parts, one for each index of `batch`. A program takes and returns all parts, laid end to end along the dimension named above; an argument that names none is the same for every part. Nothing has to cross between parts.
All inputs are finite; a program needn't handle non-finite values.
Results may differ from a plain program's by a relative error of at most 0.008.
Values may be sent and summed in bfloat16 or wider, within the bound.
No kernel may reach another device: no remote copies, remote signals or barrier semaphores. Data moves between devices by JAX's collectives and lax.ppermute only.
A program may use at most 128 MiB of HBM per device.

v0:
```python
import functools

import jax
import jax.numpy as jnp
from jax import lax
from jax.experimental import pallas as pl
from jax.experimental.pallas import tpu as pltpu
from jax.sharding import Mesh
from jax.sharding import PartitionSpec as P

AXES = ("y_hi", "z", "x", "y_lo", "core")
SEQ = ("x", "y_lo", "core")
XN, YN, ZN, CN = 4, 4, 8, 2
VMEM_LIMIT = 24 * 1024 * 1024
EDGE = 16
TILE = 512
PARTS = (12, 10, 10)
SOURCES = (6, 6, 6)
PIECES = 32
FIRST_HALF = 20
ROWS = 128
AWAY = 128
TOKEN = jax.ShapeDtypeStruct((8, 128), jnp.float32)
INV_SQRT2 = 0.7071067811865476


def core_swap(value):
    return lax.ppermute(value, "core", [(0, 1), (1, 0)])


def x_shift(value):
    route = []
    for x in range(XN):
        route += [(x * 2, (x + 1) % XN * 2), (x * 2 + 1, (x - 1) % XN * 2 + 1)]
    return lax.ppermute(value, ("x", "core"), route)


def y_shift(value):
    route = []
    for y in range(YN):
        route += [(y * 2, (y + 1) % YN * 2), (y * 2 + 1, (y - 1) % YN * 2 + 1)]
    return lax.ppermute(value, ("y_hi", "y_lo", "core"), route)


def z_shift(value):
    route = []
    for z in range(ZN):
        route += [(z * 2, (z + 1) % ZN * 2), (z * 2 + 1, (z - 1) % ZN * 2 + 1)]
    return lax.ppermute(value, ("z", "core"), route)


def fence_kernel(count, *refs):
    for source, target in zip(refs[:count], refs[-count:]):
        target[...] = source[...]


def fence(token, *values):
    inside = pl.BlockSpec(memory_space=pltpu.VMEM)
    operands = values if token is None else (*values, token)
    return pl.pallas_call(
        functools.partial(fence_kernel, len(values)),
        out_shape=[jax.ShapeDtypeStruct(v.shape, v.dtype) for v in values],
        in_specs=[inside] * len(operands),
        out_specs=[inside] * len(values),
        input_output_aliases={i: i for i in range(len(values))},
        compiler_params=pltpu.CompilerParams(vmem_limit_bytes=8 * 1024 * 1024),
        name="fence",
    )(*operands)


def edge_tile(after, before):
    width = after.shape[1]
    edge = lax.broadcasted_iota(jnp.int32, (EDGE, width), 0)
    tile = jnp.where(edge == 0, after, jnp.where(edge == EDGE - 1, before, 0.0))
    return tile.astype(jnp.bfloat16)


def halve_kernel(place_ref, shard_ref, out_ref):
    half = out_ref.shape[1]
    odd = lax.rem(place_ref[FIRST_HALF], 2)

    @pl.when(odd == 0)
    def _():
        out_ref[...] = shard_ref[:, pl.ds(0, half), :]

    @pl.when(odd == 1)
    def _():
        out_ref[...] = shard_ref[:, pl.ds(half, half), :]


def halve(place, shard):
    taps, rows, columns = shard.shape
    inside = pl.BlockSpec(memory_space=pltpu.VMEM)
    return pl.pallas_call(
        halve_kernel,
        out_shape=jax.ShapeDtypeStruct((taps, rows // 2, columns), shard.dtype),
        in_specs=[pl.BlockSpec(memory_space=pltpu.SMEM), inside],
        out_specs=inside,
        compiler_params=pltpu.CompilerParams(vmem_limit_bytes=8 * 1024 * 1024),
        name="halve",
    )(place, shard)


def order_kernel(place_ref, reverse_ref, *refs):
    move_refs, flipped_ref, token_ref = refs[:3], refs[3], refs[4]
    token_ref[...] = jnp.zeros_like(token_ref)
    rows, width = reverse_ref.shape
    part = width // PIECES
    begin = 0
    for move_ref, count in zip(move_refs, PARTS):
        size = count * part
        lane = lax.broadcasted_iota(jnp.int32, (1, size), 1)
        wanted = jnp.zeros((1, size), jnp.int32)
        for block in range(count):
            inside = (lane >= block * part) & (lane < (block + 1) * part)
            wanted = jnp.where(inside, lane + (place_ref[begin + block] - block) * part, wanted)
        source = lax.broadcasted_iota(jnp.int32, (width, size), 0)
        move_ref[...] = jnp.where(source == wanted, 1.0, 0.0).astype(jnp.bfloat16)
        begin += count
    row = lax.broadcasted_iota(jnp.int32, (rows, rows), 0)
    column = lax.broadcasted_iota(jnp.int32, (rows, rows), 1)
    flip = jnp.where(row + column == rows - 1, 1.0, 0.0).astype(jnp.bfloat16)
    flipped = jnp.dot(flip, reverse_ref[...], preferred_element_type=jnp.float32)
    flipped_ref[...] = flipped.astype(jnp.bfloat16)


def order(place, reverse_embed):
    rows, width = reverse_embed.shape
    part = width // PIECES
    inside = pl.BlockSpec(memory_space=pltpu.VMEM)
    outs = pl.pallas_call(
        order_kernel,
        out_shape=[jax.ShapeDtypeStruct((width, count * part), jnp.bfloat16) for count in PARTS]
        + [jax.ShapeDtypeStruct((rows, width), jnp.bfloat16), TOKEN],
        in_specs=[pl.BlockSpec(memory_space=pltpu.SMEM), inside],
        out_specs=[inside] * 5,
        compiler_params=pltpu.CompilerParams(vmem_limit_bytes=VMEM_LIMIT),
        cost_estimate=pl.CostEstimate(
            flops=16 * rows * width * width, bytes_accessed=8 * rows * width, transcendentals=0
        ),
        name="order",
    )(place, reverse_embed)
    return outs[:3], outs[3], outs[4]


def edge_tile(after, before):
    width = after.shape[1]
    edge = lax.broadcasted_iota(jnp.int32, (EDGE, width), 0)
    tile = jnp.where(edge == 0, after, jnp.where(edge == EDGE - 1, before, 0.0))
    return tile.astype(jnp.bfloat16)


def prepare_kernel(forward_ref, flipped_ref, low_ref, high_ref, *refs):
    move_refs, x_refs, y_refs, (away_ref, token_ref, edge_ref) = (
        refs[:3], refs[3:6], refs[6:9], refs[9:],
    )
    token_ref[...] = jnp.zeros_like(token_ref)
    rows = forward_ref.shape[0]
    kept = rows - AWAY
    low = low_ref[...].astype(jnp.float32)
    high = high_ref[...].astype(jnp.float32)
    next_row = flipped_ref[pl.ds(kept, EDGE), :].astype(jnp.float32)[0:1]
    past_row = flipped_ref[pl.ds(kept - EDGE, EDGE), :].astype(jnp.float32)[EDGE - 1 :]
    away_ref[:AWAY, :] = flipped_ref[pl.ds(kept, AWAY), :]
    away_ref[AWAY:, :] = edge_tile(low[1:2], past_row)
    edge_ref[:EDGE, :] = edge_tile(high[0:1], low[0:1])
    edge_ref[EDGE:, :] = edge_tile(next_row, high[1:2])
    for x_ref, y_ref, move_ref in zip(x_refs, y_refs, move_refs):
        edges = jnp.dot(edge_ref[...], move_ref[...], preferred_element_type=jnp.float32)
        edges = edges.astype(jnp.bfloat16)
        x_ref[:rows, :] = jnp.dot(
            forward_ref[...], move_ref[...], preferred_element_type=jnp.float32
        ).astype(jnp.bfloat16)
        x_ref[rows:, :] = edges[:EDGE]
        y_ref[:kept, :] = jnp.dot(
            flipped_ref[pl.ds(0, kept), :], move_ref[...], preferred_element_type=jnp.float32
        ).astype(jnp.bfloat16)
        y_ref[kept:, :] = edges[EDGE:]


def prepare(forward_embed, flipped, low, high, moves):
    rows, width = forward_embed.shape
    kept = rows - AWAY
    part = width // PIECES
    inside = pl.BlockSpec(memory_space=pltpu.VMEM)

    def stripes(height):
        return [jax.ShapeDtypeStruct((height, count * part), jnp.bfloat16) for count in PARTS]

    outs = pl.pallas_call(
        prepare_kernel,
        out_shape=stripes(rows + EDGE)
        + stripes(kept + EDGE)
        + [jax.ShapeDtypeStruct((AWAY + EDGE, width), jnp.bfloat16), TOKEN],
        in_specs=[inside] * 7,
        out_specs=[inside] * 8,
        scratch_shapes=[pltpu.VMEM((2 * EDGE, width), jnp.bfloat16)],
        compiler_params=pltpu.CompilerParams(vmem_limit_bytes=VMEM_LIMIT),
        cost_estimate=pl.CostEstimate(flops=1000, bytes_accessed=1000, transcendentals=0),
        name="prepare",
    )(forward_embed, flipped, low, high, *moves)
    return list(zip(outs[:3], outs[3:6])), outs[6], outs[7]


def convolve(x, flipped, blocks, columns):
    rows = x.shape[0] - EDGE
    total = None
    for tap in range(3):
        weight = jnp.concatenate([block[tap, :, columns] for block in blocks], axis=0)
        value = jnp.dot(x, weight, preferred_element_type=jnp.float32)
        shift = tap - 1 if flipped else 1 - tap
        if shift:
            value = pltpu.roll(value, shift % (rows + EDGE), 0)
        value = value[:rows]
        total = value if total is None else total + value
    return total


def partial_kernel(count, first, *refs):
    strands, blocks, refs = refs[:2], refs[2 : 2 + count], refs[2 + count :]
    out_refs, token_ref = refs[-3:-1], refs[-1]
    token_ref[...] = jnp.zeros_like(token_ref)
    @pl.loop(0, out_refs[0].shape[1] // TILE)
    def _(tile):
        columns = pl.ds(pl.multiple_of(tile * TILE, TILE), TILE)
        for strand in range(2):
            acc = convolve(strands[strand][...], strand == 1, blocks, columns)
            if not first:
                acc = acc + refs[strand][:, columns]
            out_refs[strand][:, columns] = acc


def partial_sum(strands, sources, prev):
    rows = [x.shape[0] - EDGE for x in strands]
    depth, channels = strands[0].shape[1], sources[0].shape[2]
    operands = [*strands, *sources] + ([] if prev is None else list(prev))
    inside = pl.BlockSpec(memory_space=pltpu.VMEM)
    last = len(operands)
    forward, reverse, token = pl.pallas_call(
        functools.partial(partial_kernel, len(sources), prev is None),
        out_shape=[jax.ShapeDtypeStruct((count, channels), jnp.float32) for count in rows]
        + [TOKEN],
        in_specs=[inside] * last,
        out_specs=[inside] * 3,
        input_output_aliases={} if prev is None else {last - 2: 0, last - 1: 1},
        compiler_params=pltpu.CompilerParams(vmem_limit_bytes=VMEM_LIMIT),
        cost_estimate=pl.CostEstimate(
            flops=6 * sum(rows) * depth * channels,
            bytes_accessed=6 * depth * channels,
            transcendentals=0,
        ),
        name="partial_sum",
    )(*operands)
    return (forward, reverse), token


def gelu(acc):
    return (0.5 * acc * (1.0 + lax.erf(acc * INV_SQRT2))).astype(jnp.bfloat16)


def predict(hidden_ref, head_ref, head_bias_ref, out_ref):
    rows = out_ref.shape[0]
    @pl.loop(0, rows // ROWS)
    def _(block):
        here = pl.ds(pl.multiple_of(block * ROWS, ROWS), ROWS)
        logits = jnp.dot(hidden_ref[here, :], head_ref[...], preferred_element_type=jnp.float32)
        logits = logits + head_bias_ref[...]
        tracks = jnp.maximum(logits, 0.0) + jnp.log1p(jnp.exp(-jnp.abs(logits)))
        out_ref[here, :] = tracks.astype(jnp.bfloat16)


def finish_kernel(flipped, count, x_ref, *refs):
    sources, refs = refs[:count], refs[count:]
    prev_ref, bias_ref, head_ref, head_bias_ref, out_ref, hidden_ref = refs
    @pl.loop(0, hidden_ref.shape[1] // TILE)
    def _(tile):
        here = pl.ds(pl.multiple_of(tile * TILE, TILE), TILE)
        acc = convolve(x_ref[...], flipped, sources, here)
        hidden_ref[:, here] = gelu(acc + prev_ref[:, here] + bias_ref[:, here])

    predict(hidden_ref, head_ref, head_bias_ref, out_ref)


def finish(flipped, x, sources, prev, bias, head, head_bias):
    rows, depth = x.shape[0] - EDGE, x.shape[1]
    channels, tracks = head.shape
    inside = pl.BlockSpec(memory_space=pltpu.VMEM)
    return pl.pallas_call(
        functools.partial(finish_kernel, flipped, len(sources)),
        out_shape=jax.ShapeDtypeStruct((rows, tracks), jnp.bfloat16),
        in_specs=[inside] * (len(sources) + 5),
        out_specs=inside,
        scratch_shapes=[pltpu.VMEM((rows, channels), jnp.bfloat16)],
        compiler_params=pltpu.CompilerParams(vmem_limit_bytes=VMEM_LIMIT),
        cost_estimate=pl.CostEstimate(
            flops=2 * rows * channels * (3 * depth + tracks),
            bytes_accessed=6 * depth * channels + 2 * channels * tracks,
            transcendentals=rows * channels,
        ),
        name="finish",
    )(x, *sources, prev, bias, head, head_bias[None])


def whole_kernel(sizes, away_ref, *refs):
    moves, refs = refs[: len(sizes)], refs[len(sizes) :]
    sources, refs = refs[: sum(sizes)], refs[sum(sizes) :]
    bias_ref, head_ref, head_bias_ref, out_ref, hidden_ref = refs
    stripes = [
        jnp.dot(away_ref[...], move[...], preferred_element_type=jnp.float32).astype(jnp.bfloat16)
        for move in moves
    ]
    @pl.loop(0, hidden_ref.shape[1] // TILE)
    def _(tile):
        here = pl.ds(pl.multiple_of(tile * TILE, TILE), TILE)
        acc, begin = bias_ref[:, here], 0
        for stripe, count in zip(stripes, sizes):
            acc = acc + convolve(stripe, True, sources[begin : begin + count], here)
            begin += count
        hidden_ref[:, here] = gelu(acc)

    predict(hidden_ref, head_ref, head_bias_ref, out_ref)


def whole(away, moves, sources, bias, head, head_bias):
    rows = away.shape[0] - EDGE
    channels, tracks = head.shape
    inside = pl.BlockSpec(memory_space=pltpu.VMEM)
    return pl.pallas_call(
        functools.partial(whole_kernel, SOURCES),
        out_shape=jax.ShapeDtypeStruct((rows, tracks), jnp.bfloat16),
        in_specs=[inside] * (len(moves) + len(sources) + 4),
        out_specs=inside,
        scratch_shapes=[pltpu.VMEM((rows, channels), jnp.bfloat16)],
        compiler_params=pltpu.CompilerParams(vmem_limit_bytes=VMEM_LIMIT),
        cost_estimate=pl.CostEstimate(
            flops=2 * rows * channels * (4 * channels + tracks),
            bytes_accessed=6 * channels * channels,
            transcendentals=rows * channels,
        ),
        name="whole",
    )(away, *moves, *sources, bias, head, head_bias[None])


def per_device(forward_embed, reverse_embed, conv_weight, conv_bias, head_weight, head_bias):
    own = conv_weight[0]
    x, y, core = lax.axis_index("x"), lax.axis_index("y_lo"), lax.axis_index("core")
    ends = XN * 2 * CN

    def seq(x_of, y_of, core_of):
        return (x_of % XN) * 4 + y_of * 2 + core_of

    step = 1 - 2 * core
    back, fore, far = x - step + XN, x + step + XN, x + 2
    other, over = 1 - core, 1 - y
    odd = lax.axis_index("z") % 2

    def both(*shards):
        return [2 * shard + half for shard in shards for half in range(2)]

    place = jnp.stack(
        both(
            seq(x, y, core), seq(x, y, other), seq(x, over, core), seq(x, over, other),
            seq(back, y, core), seq(fore, y, other),
            seq(back, over, core), seq(fore, over, other), seq(far, y, core), seq(far, y, other),
        )
        + [2 * seq(back, y, other) + odd, 2 * seq(fore, y, core) + odd]
        + [2 * seq(back, y, other) + 1 - odd, 2 * seq(fore, y, core) + 1 - odd]
        + both(
            seq(back, over, other), seq(fore, over, core),
            seq(far, over, core), seq(far, over, other),
        )
    ).astype(jnp.int32)

    with jax.named_scope("near"):
        near = x_shift(own)
    with jax.named_scope("across"):
        across = y_shift(own)
    with jax.named_scope("sibling"):
        sibling = core_swap(own)
    sibling_half = halve(place, sibling)
    with jax.named_scope("second"):
        second = x_shift(sibling_half)
    up = [(i, i + 1) for i in range(ends - 1)]
    down = [(b, a) for a, b in up]
    with jax.named_scope("low"):
        low = lax.ppermute(jnp.stack([forward_embed[-1], reverse_embed[-1]]), SEQ, up)
    with jax.named_scope("high"):
        high = lax.ppermute(jnp.stack([forward_embed[0], reverse_embed[0]]), SEQ, down)
    moves, flipped, token = order(place, reverse_embed)
    near, across, low, high = fence(token, near, across, low, high)

    with jax.named_scope("distant"):
        distant = x_shift(near)
    with jax.named_scope("near_over"):
        near_over = y_shift(near)
    with jax.named_scope("across_b"):
        across_b = core_swap(across)
    with jax.named_scope("near_b"):
        near_b = core_swap(near)
    (x_1, x_2, x_3), away, token = prepare(forward_embed, flipped, low, high, moves)
    shards_1 = [own, sibling, across, across_b, near, near_b]
    acc, token = partial_sum(x_1, shards_1, None)
    distant, near_over, across_b, second = fence(token, distant, near_over, across_b, second)
    shards_1[3] = across_b

    with jax.named_scope("second_z"):
        second_z = z_shift(second)
    with jax.named_scope("second_over"):
        second_over = x_shift(across_b)
    with jax.named_scope("distant_over"):
        distant_over = y_shift(distant)
    with jax.named_scope("near_over_b"):
        near_over_b = core_swap(near_over)
    with jax.named_scope("distant_b"):
        distant_b = core_swap(distant)
    with jax.named_scope("second_b"):
        second_b = core_swap(second)
    shards_2 = [near_over, near_over_b, distant, distant_b, second, second_b]
    acc, token = partial_sum(x_2, shards_2, acc)
    second_over, distant_over, second_z, away = fence(
        token, second_over, distant_over, second_z, away
    )

    mirror = [(i, ends - 1 - i) for i in range(ends)]
    with jax.named_scope("away"):
        away = lax.ppermute(away, SEQ, mirror)
    with jax.named_scope("second_over_b"):
        second_over_b = core_swap(second_over)
    with jax.named_scope("distant_over_b"):
        distant_over_b = core_swap(distant_over)
    with jax.named_scope("second_z_b"):
        second_z_b = core_swap(second_z)
    shards_3 = [second_z, second_z_b, second_over, second_over_b, distant_over, distant_over_b]
    rest = (conv_bias, head_weight, head_bias)
    reverse_tracks = finish(True, x_3[1], shards_3, acc[1], *rest)
    with jax.named_scope("mirrored"):
        mirrored = lax.ppermute(reverse_tracks, SEQ, mirror)
    forward_tracks = finish(False, x_3[0], shards_3, acc[0], *rest)
    away_tracks = whole(away, moves, shards_1 + shards_2 + shards_3, *rest)
    reverse = jnp.concatenate([mirrored, away_tracks])
    mean = 0.5 * (forward_tracks.astype(jnp.float32) + reverse.astype(jnp.float32))
    return mean.astype(jnp.bfloat16)


def solution(mesh):
    fine = Mesh(mesh.devices.reshape(2, 8, XN, 2, CN), AXES)
    return jax.shard_map(
        per_device,
        mesh=fine,
        in_specs=(
            P(AXES, None),
            P(AXES, None),
            P(None, None, SEQ, None),
            P(),
            P(),
            P(),
        ),
        out_specs=P(AXES, None),
        check_vma=False,
    )
```

profile of v0, /device:TPU:1, one launch (start us, length us, event | category | flops | bytes accessed | tf_op | source)
XLA Modules:
  0.0 81.8 jit_solution(9838410134959130571)
XLA Ops:
  0.0 3.3 %collective-permute-start = (bf16[3,96,1536]{2,1,0:T(8,128)(2,1)}, bf16[3,96,1536]{2,1,0:T(8,128)(2,1)S(1)}, u32[]{:S(2)}, u32[]{:S(2)}) collective-permute-start(bf16[3,96,1536]{2,1,0:T(8,128)(2,1)} %bitcast.34), channel_id=1, source_target_pairs={{0,4},{1,13},{4,8},{5,1},{8,12},{9,5},{12,0},{13,9},{2,6},{3,15},{... | collective-permute-start | bytes 2654216 | tf_op jit(solution)/shard_map/near/ppermute | solution.py:35
  3.3 2.7 %collective-permute-start.1 = (bf16[3,96,1536]{2,1,0:T(8,128)(2,1)}, bf16[3,96,1536]{2,1,0:T(8,128)(2,1)S(1)}, u32[]{:S(2)}, u32[]{:S(2)}) collective-permute-start(bf16[3,96,1536]{2,1,0:T(8,128)(2,1)} %bitcast.35), channel_id=1, source_target_pairs={{0,2},{1,131},{2,128},{3,1},{128,130},{129,3},{130,0},{131,129},{4... | collective-permute-start | bytes 2654216 | tf_op jit(solution)/shard_map/across/ppermute | solution.py:42
  6.0 0.8 fusion
  6.9 1.9 %collective-permute-start.2 = (bf16[2,1536]{1,0:T(2,128)(2,1)S(1)}, bf16[2,1536]{1,0:T(2,128)(2,1)S(1)}, u32[]{:S(2)}, u32[]{:S(2)}) collective-permute-start(bf16[2,1536]{1,0:T(2,128)(2,1)S(1)} %pad_maximum_fusion), channel_id=1, source_target_pairs={{0,1},{1,2},{2,3},{3,4},{4,5},{5,6},{6,7},{7,8},{8,9},{9,10},{10,1... | collective-permute-start | bytes 18440 | tf_op jit(solution)/shard_map/low/ppermute | solution.py:386
  8.8 2.4 %collective-permute-start.3 = (bf16[2,1536]{1,0:T(2,128)(2,1)S(1)}, bf16[2,1536]{1,0:T(2,128)(2,1)S(1)}, u32[]{:S(2)}, u32[]{:S(2)}) collective-permute-start(bf16[2,1536]{1,0:T(2,128)(2,1)S(1)} %pad_maximum_fusion.1), channel_id=1, source_target_pairs={{1,0},{2,1},{3,2},{4,3},{5,4},{6,5},{7,6},{8,7},{9,8},{10,9},{11,1... | collective-permute-start | bytes 18440 | tf_op jit(solution)/shard_map/high/ppermute | solution.py:388
  11.3 0.1 stack.137.place_ref
  11.4 0.0 copy-start.5
  11.5 1.3 %copy-done.5 = bf16[384,1536]{1,0:T(8,128)(2,1)S(1)} copy-done((bf16[384,1536]{1,0:T(8,128)(2,1)S(1)}, bf16[384,1536]{1,0:T(8,128)(2,1)}, u32[]{:S(2)}) %copy-start.5) | copy-done | bytes 1179672
  12.7 3.1 %order.1 = (bf16[1536,576]{1,0:T(8,128)(2,1)S(1)}, bf16[1536,480]{1,0:T(8,128)(2,1)S(1)}, bf16[1536,480]{1,0:T(8,128)(2,1)S(1)}, bf16[384,1536]{1,0:T(8,128)(2,1)S(1)}, f32[8,128]{1,0:T(8,128)S(1)}) custom-call(s32[32]{0:T(128)S(1)} %stack.137.place_ref, bf16[384,1536]{1,0:T(8,128)(2,1)S(1)} %copy-done.5), custom_call_target="tpu_custom_call" | custom-call | flops 14495514624 | bytes 4718592 | tf_op jit(solution)/shard_map/order/pallas_call | solution.py:131
  15.8 0.0 copy-start.1
  15.8 0.0 collective-permute-done.3.refs_3_
  15.8 0.0 collective-permute-done.refs_0_
  15.9 0.5 collective-permute-done.1.refs_1_
  16.3 0.2 fence.3
  16.6 1.4 %collective-permute-start.6 = (bf16[3,96,1536]{2,1,0:T(8,128)(2,1)S(1)}, bf16[3,96,1536]{2,1,0:T(8,128)(2,1)S(1)}, u32[]{:S(2)}, u32[]{:S(2)}) collective-permute-start(bf16[3,96,1536]{2,1,0:T(8,128)(2,1)S(1)} %get-tuple-element.44.refs_4_.refs_5_), channel_id=1, source_target_pairs={{0,1},{1,0},{2,3},{3,2},{4,5},{5,4},{6,7},{7,6},{8,9},{9,8},{10,11... | collective-permute-start | bytes 2654216 | tf_op jit(solution)/shard_map/across_b/ppermute | solution.py:28
  18.0 0.1 collective-permute-start.9
  18.1 3.0 %collective-permute-start.4 = (bf16[3,96,1536]{2,1,0:T(8,128)(2,1)S(1)}, bf16[3,96,1536]{2,1,0:T(8,128)(2,1)S(1)}, u32[]{:S(2)}, u32[]{:S(2)}) collective-permute-start(bf16[3,96,1536]{2,1,0:T(8,128)(2,1)S(1)} %get-tuple-element.43.refs_6_.refs_7_), channel_id=1, source_target_pairs={{0,4},{1,13},{4,8},{5,1},{8,12},{9,5},{12,0},{13,9},{2,6},{3,15},{... | collective-permute-start | bytes 2654216 | tf_op jit(solution)/shard_map/distant/ppermute | solution.py:35
  21.1 0.0 collective-permute-start.5
  21.1 0.0 collective-permute-done.7.shard_ref.refs_3_.refs_4_
  21.1 0.6 halve.1
  21.7 1.4 %collective-permute-start.8 = (bf16[3,48,1536]{2,1,0:T(8,128)(2,1)S(1)}, bf16[3,48,1536]{2,1,0:T(8,128)(2,1)S(1)}, u32[]{:S(2)}, u32[]{:S(2)}) collective-permute-start(bf16[3,48,1536]{2,1,0:T(8,128)(2,1)S(1)} %halve.1), channel_id=1, source_target_pairs={{0,4},{1,13},{4,8},{5,1},{8,12},{9,5},{12,0},{13,9},{2,6},{3,15},{... | collective-permute-start | bytes 1327112 | tf_op jit(solution)/shard_map/second/ppermute | solution.py:35
  23.1 5.0 %prepare.1 = (bf16[400,576]{1,0:T(8,128)(2,1)S(1)}, bf16[400,480]{1,0:T(8,128)(2,1)S(1)}, bf16[400,480]{1,0:T(8,128)(2,1)S(1)}, bf16[272,576]{1,0:T(8,128)(2,1)S...) custom-call(bf16[384,1536]{1,0:T(8,128)(2,1)S(1)} %copy-done.1, ...), custom_call_target="tpu_custom_call" | custom-call | flops 1000 | bytes 1000 | tf_op jit(solution)/shard_map/prepare/pallas_call | solution.py:190
  28.1 5.4 %partial_sum.2 = (f32[384,1536]{1,0:T(8,128)S(1)}, f32[256,1536]{1,0:T(8,128)S(1)}, f32[8,128]{1,0:T(8,128)S(1)}) custom-call(bf16[400,576]{1,0:T(8,128)(2,1)S(1)} %get-tuple-element.45.refs_0_, bf16[272,576]{1,0:T(8,128)(2,1)S(1)} %get-tuple-element.46.refs_1_, bf16[3,96,1536]{2,1,0:T(8,128)(2,1)S(1)} %bitcast.37, ...), custom_call_target="tpu_custom_call" | custom-call | flops 3397386240 | bytes 5308416 | tf_op jit(solution)/shard_map/partial_sum/pallas_call | solution.py:239
  33.6 2.2 %collective-permute-done.8.refs_3_ = bf16[3,48,1536]{2,1,0:T(8,128)(2,1)S(1)} collective-permute-done((bf16[3,48,1536]{2,1,0:T(8,128)(2,1)S(1)}, bf16[3,48,1536]{2,1,0:T(8,128)(2,1)S(1)}, u32[]{:S(2)}, u32[]{:S(2)}) %collective-permute-start.8) | collective-permute-done | bytes 442400 | tf_op jit(solution)/shard_map/second/ppermute | solution.py:35
  35.8 0.4 fence.4
  36.2 1.8 %collective-permute-start.13 = (bf16[3,96,1536]{2,1,0:T(8,128)(2,1)S(1)}, bf16[3,96,1536]{2,1,0:T(8,128)(2,1)S(1)}, u32[]{:S(2)}, u32[]{:S(2)}) collective-permute-start(bf16[3,96,1536]{2,1,0:T(8,128)(2,1)S(1)} %get-tuple-element.54.refs_2_.refs_9_), channel_id=1, source_target_pairs={{0,1},{1,0},{2,3},{3,2},{4,5},{5,4},{6,7},{7,6},{8,9},{9,8},{10,11... | collective-permute-start | bytes 2654216 | tf_op jit(solution)/shard_map/near_over_b/ppermute | solution.py:28
  38.0 0.1 collective-permute-start.14
  38.1 0.4 collective-permute-start.15
  38.5 1.7 %collective-permute-start.10 = (bf16[3,96,1536]{2,1,0:T(8,128)(2,1)S(1)}, bf16[3,96,1536]{2,1,0:T(8,128)(2,1)S(1)}, u32[]{:S(2)}, u32[]{:S(2)}) collective-permute-start(bf16[3,96,1536]{2,1,0:T(8,128)(2,1)S(1)} %get-tuple-element.48.refs_6_), channel_id=1, source_target_pairs={{0,4},{1,13},{4,8},{5,1},{8,12},{9,5},{12,0},{13,9},{2,6},{3,15},{... | collective-permute-start | bytes 2654216 | tf_op jit(solution)/shard_map/second_over/ppermute | solution.py:35
  40.2 0.0 collective-permute-start.11
  40.2 1.7 %collective-permute-done.15.refs_7_.refs_14_ = bf16[3,48,1536]{2,1,0:T(8,128)(2,1)S(1)} collective-permute-done((bf16[3,48,1536]{2,1,0:T(8,128)(2,1)S(1)}, bf16[3,48,1536]{2,1,0:T(8,128)(2,1)S(1)}, u32[]{:S(2)}, u32[]{:S(2)}) %collective-permute-start.15) | collective-permute-done | bytes 442400 | tf_op jit(solution)/shard_map/second_b/ppermute | solution.py:28
  41.9 5.3 %collective-permute-start.12 = (bf16[3,48,1536]{2,1,0:T(8,128)(2,1)S(1)}, bf16[3,48,1536]{2,1,0:T(8,128)(2,1)S(1)}, u32[]{:S(2)}, u32[]{:S(2)}) collective-permute-start(bf16[3,48,1536]{2,1,0:T(8,128)(2,1)S(1)} %get-tuple-element.50.refs_6_.refs_13_), channel_id=1, source_target_pairs={{0,16},{1,113},{16,32},{17,1},{32,48},{33,17},{48,64},{49,33},{64,... | collective-permute-start | bytes 1327112 | tf_op jit(solution)/shard_map/second_z/ppermute | solution.py:49
  47.3 3.9 %partial_sum.3 = (f32[384,1536]{1,0:T(8,128)S(1)}, f32[256,1536]{1,0:T(8,128)S(1)}, f32[8,128]{1,0:T(8,128)S(1)}) custom-call(bf16[400,480]{1,0:T(8,128)(2,1)S(1)} %get-tuple-element.52.refs_0_, bf16[272,480]{1,0:T(8,128)(2,1)S(1)} %get-tuple-element.53.refs_1_, ...), custom_call_target="tpu_custom_call", output_to_operand_aliasing={{0}: (8, {}), {1}: (9, {})} | custom-call | flops 2831155200 | bytes 4423680 | tf_op jit(solution)/shard_map/partial_sum/pallas_call | solution.py:239
  51.1 0.0 copy-start.3
  51.2 0.0 copy-start.4
  51.2 1.3 %collective-permute-done.12.refs_2_ = bf16[3,48,1536]{2,1,0:T(8,128)(2,1)S(1)} collective-permute-done((bf16[3,48,1536]{2,1,0:T(8,128)(2,1)S(1)}, bf16[3,48,1536]{2,1,0:T(8,128)(2,1)S(1)}, u32[]{:S(2)}, u32[]{:S(2)}) %collective-permute-start.12) | collective-permute-done | bytes 442400 | tf_op jit(solution)/shard_map/second_z/ppermute | solution.py:49
  52.5 0.3 fence.5
  52.8 1.8 %collective-permute-start.17 = (bf16[3,96,1536]{2,1,0:T(8,128)(2,1)S(1)}, bf16[3,96,1536]{2,1,0:T(8,128)(2,1)S(1)}, u32[]{:S(2)}, u32[]{:S(2)}) collective-permute-start(bf16[3,96,1536]{2,1,0:T(8,128)(2,1)S(1)} %get-tuple-element.59.refs_2_.refs_17_), channel_id=1, source_target_pairs={{0,1},{1,0},{2,3},{3,2},{4,5},{5,4},{6,7},{7,6},{8,9},{9,8},{10,11... | collective-permute-start | bytes 2654216 | tf_op jit(solution)/shard_map/second_over_b/ppermute | solution.py:28
  54.6 0.1 collective-permute-start.18
  54.7 0.4 collective-permute-start.16
  55.1 0.6 collective-permute-start.20
  55.7 2.8 %collective-permute-done.16.refs_1_.refs_16_ = bf16[3,48,1536]{2,1,0:T(8,128)(2,1)S(1)} collective-permute-done((bf16[3,48,1536]{2,1,0:T(8,128)(2,1)S(1)}, bf16[3,48,1536]{2,1,0:T(8,128)(2,1)S(1)}, u32[]{:S(2)}, u32[]{:S(2)}) %collective-permute-start.16) | collective-permute-done | bytes 442400 | tf_op jit(solution)/shard_map/second_z_b/ppermute | solution.py:28
  58.6 3.9 %finish.3 = bf16[256,1024]{1,0:T(8,128)(2,1)S(1)} custom-call(bf16[272,480]{1,0:T(8,128)(2,1)S(1)} %get-tuple-element.62.x_ref, bf16[3,48,1536]{2,1,0:T(8,128)(2,1)S(1)} %get-tuple-element.58.refs_0_.refs_15_, bf16[3,48,1536]{2,1,0:T(8,128)(2,1)S(1)} %collective-permute-done.16.refs_1_.refs_16_, bf16[3,96,1536]{2,1,0:T(8,128)(2,1)S(1)} %get-tuple-element.59.refs_2_.refs_17_, ...), custom_call_target="tpu_custom_call" | custom-call | flops 1937768448 | bytes 7569408 | tf_op jit(solution)/shard_map/finish/pallas_call | solution.py:288
  62.5 1.0 %collective-permute-start.19 = (bf16[256,1024]{1,0:T(8,128)(2,1)S(1)}, bf16[256,1024]{1,0:T(8,128)(2,1)S(1)}, u32[]{:S(2)}, u32[]{:S(2)}) collective-permute-start(bf16[256,1024]{1,0:T(8,128)(2,1)S(1)} %finish.3), channel_id=1, source_target_pairs={{0,15},{1,14},{2,13},{3,12},{4,11},{5,10},{6,9},{7,8},{8,7},{9,6},... | collective-permute-start | bytes 1572872 | tf_op jit(solution)/shard_map/mirrored/ppermute | solution.py:437
  63.5 6.5 %collective-permute-done.20.away_ref = bf16[144,1536]{1,0:T(8,128)(2,1)S(1)} collective-permute-done((bf16[144,1536]{1,0:T(8,128)(2,1)S(1)}, bf16[144,1536]{1,0:T(8,128)(2,1)S(1)}, u32[]{:S(2)}, u32[]{:S(2)}) %collective-permute-start.20) | collective-permute-done | bytes 442400 | tf_op jit(solution)/shard_map/away/ppermute | solution.py:426
  69.9 4.9 %whole.1 = bf16[128,1024]{1,0:T(8,128)(2,1)S(1)} custom-call(bf16[144,1536]{1,0:T(8,128)(2,1)S(1)} %collective-permute-done.20.away_ref, bf16[1536,576]{1,0:T(8,128)(2,1)S(1)} %get-tuple-element.39.refs_0_, bf16[1536,480]{1,0:T(8,128)(2,1)S(1)} %get-tuple-element.40.refs_1_, bf16[1536,480]{1,0:T(8,128)(2,1)S(1)} %get-tuple-element.41.refs_2_, ...), custom_call_target="tpu_custom_call" | custom-call | flops 2818572288 | bytes 14155776 | tf_op jit(solution)/shard_map/whole/pallas_call | solution.py:328
  74.9 5.7 %finish.2 = bf16[384,1024]{1,0:T(8,128)(2,1)S(1)} custom-call(bf16[400,480]{1,0:T(8,128)(2,1)S(1)} %get-tuple-element.42.x_ref, bf16[3,48,1536]{2,1,0:T(8,128)(2,1)S(1)} %get-tuple-element.58.refs_0_.refs_15_, bf16[3,48,1536]{2,1,0:T(8,128)(2,1)S(1)} %collective-permute-done.16.refs_1_.refs_16_, bf16[3,96,1536]{2,1,0:T(8,128)(2,1)S(1)} %get-tuple-element.59.refs_2_.refs_17_, ...), custom_call_target="tpu_custom_call" | custom-call | flops 2906652672 | bytes 7569408 | tf_op jit(solution)/shard_map/finish/pallas_call | solution.py:288
  80.6 1.2 %multiply_convert_fusion = bf16[384,1024]{1,0:T(8,128)(2,1)} fusion(bf16[384,1024]{1,0:T(8,128)(2,1)S(1)} %finish.2, bf16[128,1024]{1,0:T(8,128)(2,1)S(1)} %whole.1, bf16[256,1024]{1,0:T(8,128)(2,1)S(1)} %collective-permute-done.19), kind=kLoop, calls=%fused_computation | loop fusion | flops 3145728 | bytes 2359296 | tf_op jit(solution)/shard_map/convert_element_type | solution.py:442
  (22 shorter events, 0.1 us)
Async XLA Ops:
  0.0 15.9 %collective-permute-start = (bf16[3,96,1536]{2,1,0:T(8,128)(2,1)}, bf16[3,96,1536]{2,1,0:T(8,128)(2,1)S(1)}, u32[]{:S(2)}, u32[]{:S(2)}) collective-permute-start(bf16[3,96,1536]{2,1,0:T(8,128)(2,1)} %bitcast.34), channel_id=1, source_target_pairs={{0,4},{1,13},{4,8},{5,1},{8,12},{9,5},{12,0},{13,9},{2,6},{3,15},{... | collective-permute-start | bytes 2654216 | tf_op jit(solution)/shard_map/near/ppermute | solution.py:35
  3.3 13.0 %collective-permute-start.1 = (bf16[3,96,1536]{2,1,0:T(8,128)(2,1)}, bf16[3,96,1536]{2,1,0:T(8,128)(2,1)S(1)}, u32[]{:S(2)}, u32[]{:S(2)}) collective-permute-start(bf16[3,96,1536]{2,1,0:T(8,128)(2,1)} %bitcast.35), channel_id=1, source_target_pairs={{0,2},{1,131},{2,128},{3,1},{128,130},{129,3},{130,0},{131,129},{4... | collective-permute-start | bytes 2654216 | tf_op jit(solution)/shard_map/across/ppermute | solution.py:42
  6.0 15.0 %collective-permute-start.7 = (bf16[3,96,1536]{2,1,0:T(8,128)(2,1)}, bf16[3,96,1536]{2,1,0:T(8,128)(2,1)S(1)}, u32[]{:S(2)}, u32[]{:S(2)}) collective-permute-start(bf16[3,96,1536]{2,1,0:T(8,128)(2,1)} %bitcast.36), channel_id=1, source_target_pairs={{0,1},{1,0},{2,3},{3,2},{4,5},{5,4},{6,7},{7,6},{8,9},{9,8},{10,11... | collective-permute-start | bytes 2654216 | tf_op jit(solution)/shard_map/sibling/ppermute | solution.py:28
  6.9 8.9 %collective-permute-start.2 = (bf16[2,1536]{1,0:T(2,128)(2,1)S(1)}, bf16[2,1536]{1,0:T(2,128)(2,1)S(1)}, u32[]{:S(2)}, u32[]{:S(2)}) collective-permute-start(bf16[2,1536]{1,0:T(2,128)(2,1)S(1)} %pad_maximum_fusion), channel_id=1, source_target_pairs={{0,1},{1,2},{2,3},{3,4},{4,5},{5,6},{6,7},{7,8},{8,9},{9,10},{10,1... | collective-permute-start | bytes 18440 | tf_op jit(solution)/shard_map/low/ppermute | solution.py:386
  8.8 7.0 %collective-permute-start.3 = (bf16[2,1536]{1,0:T(2,128)(2,1)S(1)}, bf16[2,1536]{1,0:T(2,128)(2,1)S(1)}, u32[]{:S(2)}, u32[]{:S(2)}) collective-permute-start(bf16[2,1536]{1,0:T(2,128)(2,1)S(1)} %pad_maximum_fusion.1), channel_id=1, source_target_pairs={{1,0},{2,1},{3,2},{4,3},{5,4},{6,5},{7,6},{8,7},{9,8},{10,9},{11,1... | collective-permute-start | bytes 18440 | tf_op jit(solution)/shard_map/high/ppermute | solution.py:388
  11.4 1.3 %copy-start.5 = (bf16[384,1536]{1,0:T(8,128)(2,1)S(1)}, bf16[384,1536]{1,0:T(8,128)(2,1)}, u32[]{:S(2)}) copy-start(bf16[384,1536]{1,0:T(8,128)(2,1)} %reverse_ref.1) | copy-start | bytes 3538948
  15.8 7.3 %copy-start.1 = (bf16[384,1536]{1,0:T(8,128)(2,1)S(1)}, bf16[384,1536]{1,0:T(8,128)(2,1)}, u32[]{:S(2)}) copy-start(bf16[384,1536]{1,0:T(8,128)(2,1)} %forward_ref.1) | copy-start | bytes 3538948
  16.6 11.6 %collective-permute-start.6 = (bf16[3,96,1536]{2,1,0:T(8,128)(2,1)S(1)}, bf16[3,96,1536]{2,1,0:T(8,128)(2,1)S(1)}, u32[]{:S(2)}, u32[]{:S(2)}) collective-permute-start(bf16[3,96,1536]{2,1,0:T(8,128)(2,1)S(1)} %get-tuple-element.44.refs_4_.refs_5_), channel_id=1, source_target_pairs={{0,1},{1,0},{2,3},{3,2},{4,5},{5,4},{6,7},{7,6},{8,9},{9,8},{10,11... | collective-permute-start | bytes 2654216 | tf_op jit(solution)/shard_map/across_b/ppermute | solution.py:28
  18.0 10.1 %collective-permute-start.9 = (bf16[3,96,1536]{2,1,0:T(8,128)(2,1)S(1)}, bf16[3,96,1536]{2,1,0:T(8,128)(2,1)S(1)}, u32[]{:S(2)}, u32[]{:S(2)}) collective-permute-start(bf16[3,96,1536]{2,1,0:T(8,128)(2,1)S(1)} %get-tuple-element.43.refs_6_.refs_7_), channel_id=1, source_target_pairs={{0,1},{1,0},{2,3},{3,2},{4,5},{5,4},{6,7},{7,6},{8,9},{9,8},{10,11... | collective-permute-start | bytes 2654216 | tf_op jit(solution)/shard_map/near_b/ppermute | solution.py:28
  18.1 17.7 %collective-permute-start.4 = (bf16[3,96,1536]{2,1,0:T(8,128)(2,1)S(1)}, bf16[3,96,1536]{2,1,0:T(8,128)(2,1)S(1)}, u32[]{:S(2)}, u32[]{:S(2)}) collective-permute-start(bf16[3,96,1536]{2,1,0:T(8,128)(2,1)S(1)} %get-tuple-element.43.refs_6_.refs_7_), channel_id=1, source_target_pairs={{0,4},{1,13},{4,8},{5,1},{8,12},{9,5},{12,0},{13,9},{2,6},{3,15},{... | collective-permute-start | bytes 2654216 | tf_op jit(solution)/shard_map/distant/ppermute | solution.py:35
  21.1 14.7 %collective-permute-start.5 = (bf16[3,96,1536]{2,1,0:T(8,128)(2,1)S(1)}, bf16[3,96,1536]{2,1,0:T(8,128)(2,1)S(1)}, u32[]{:S(2)}, u32[]{:S(2)}) collective-permute-start(bf16[3,96,1536]{2,1,0:T(8,128)(2,1)S(1)} %get-tuple-element.43.refs_6_.refs_7_), channel_id=1, source_target_pairs={{0,2},{1,131},{2,128},{3,1},{128,130},{129,3},{130,0},{131,129},{4... | collective-permute-start | bytes 2654216 | tf_op jit(solution)/shard_map/near_over/ppermute | solution.py:42
  21.7 14.1 %collective-permute-start.8 = (bf16[3,48,1536]{2,1,0:T(8,128)(2,1)S(1)}, bf16[3,48,1536]{2,1,0:T(8,128)(2,1)S(1)}, u32[]{:S(2)}, u32[]{:S(2)}) collective-permute-start(bf16[3,48,1536]{2,1,0:T(8,128)(2,1)S(1)} %halve.1), channel_id=1, source_target_pairs={{0,4},{1,13},{4,8},{5,1},{8,12},{9,5},{12,0},{13,9},{2,6},{3,15},{... | collective-permute-start | bytes 1327112 | tf_op jit(solution)/shard_map/second/ppermute | solution.py:35
  23.1 5.0 %copy-start.2 = (bf16[1,3,96,1536]{3,2,1,0:T(8,128)(2,1)S(1)}, bf16[1,3,96,1536]{3,2,1,0:T(8,128)(2,1)}, u32[]{:S(2)}) copy-start(bf16[1,3,96,1536]{3,2,1,0:T(8,128)(2,1)} %param.8) | copy-start | bytes 2654212
  36.2 11.1 %collective-permute-start.13 = (bf16[3,96,1536]{2,1,0:T(8,128)(2,1)S(1)}, bf16[3,96,1536]{2,1,0:T(8,128)(2,1)S(1)}, u32[]{:S(2)}, u32[]{:S(2)}) collective-permute-start(bf16[3,96,1536]{2,1,0:T(8,128)(2,1)S(1)} %get-tuple-element.54.refs_2_.refs_9_), channel_id=1, source_target_pairs={{0,1},{1,0},{2,3},{3,2},{4,5},{5,4},{6,7},{7,6},{8,9},{9,8},{10,11... | collective-permute-start | bytes 2654216 | tf_op jit(solution)/shard_map/near_over_b/ppermute | solution.py:28
  38.0 9.3 %collective-permute-start.14 = (bf16[3,96,1536]{2,1,0:T(8,128)(2,1)S(1)}, bf16[3,96,1536]{2,1,0:T(8,128)(2,1)S(1)}, u32[]{:S(2)}, u32[]{:S(2)}) collective-permute-start(bf16[3,96,1536]{2,1,0:T(8,128)(2,1)S(1)} %get-tuple-element.49.refs_4_.refs_11_), channel_id=1, source_target_pairs={{0,1},{1,0},{2,3},{3,2},{4,5},{5,4},{6,7},{7,6},{8,9},{9,8},{10,11... | collective-permute-start | bytes 2654216 | tf_op jit(solution)/shard_map/distant_b/ppermute | solution.py:28
  38.1 3.9 %collective-permute-start.15 = (bf16[3,48,1536]{2,1,0:T(8,128)(2,1)S(1)}, bf16[3,48,1536]{2,1,0:T(8,128)(2,1)S(1)}, u32[]{:S(2)}, u32[]{:S(2)}) collective-permute-start(bf16[3,48,1536]{2,1,0:T(8,128)(2,1)S(1)} %get-tuple-element.50.refs_6_.refs_13_), channel_id=1, source_target_pairs={{0,1},{1,0},{2,3},{3,2},{4,5},{5,4},{6,7},{7,6},{8,9},{9,8},{10,11... | collective-permute-start | bytes 1327112 | tf_op jit(solution)/shard_map/second_b/ppermute | solution.py:28
  38.5 14.0 %collective-permute-start.10 = (bf16[3,96,1536]{2,1,0:T(8,128)(2,1)S(1)}, bf16[3,96,1536]{2,1,0:T(8,128)(2,1)S(1)}, u32[]{:S(2)}, u32[]{:S(2)}) collective-permute-start(bf16[3,96,1536]{2,1,0:T(8,128)(2,1)S(1)} %get-tuple-element.48.refs_6_), channel_id=1, source_target_pairs={{0,4},{1,13},{4,8},{5,1},{8,12},{9,5},{12,0},{13,9},{2,6},{3,15},{... | collective-permute-start | bytes 2654216 | tf_op jit(solution)/shard_map/second_over/ppermute | solution.py:35
  40.2 12.3 %collective-permute-start.11 = (bf16[3,96,1536]{2,1,0:T(8,128)(2,1)S(1)}, bf16[3,96,1536]{2,1,0:T(8,128)(2,1)S(1)}, u32[]{:S(2)}, u32[]{:S(2)}) collective-permute-start(bf16[3,96,1536]{2,1,0:T(8,128)(2,1)S(1)} %get-tuple-element.49.refs_4_.refs_11_), channel_id=1, source_target_pairs={{0,2},{1,131},{2,128},{3,1},{128,130},{129,3},{130,0},{131,129},{4... | collective-permute-start | bytes 2654216 | tf_op jit(solution)/shard_map/distant_over/ppermute | solution.py:42
  41.9 10.6 %collective-permute-start.12 = (bf16[3,48,1536]{2,1,0:T(8,128)(2,1)S(1)}, bf16[3,48,1536]{2,1,0:T(8,128)(2,1)S(1)}, u32[]{:S(2)}, u32[]{:S(2)}) collective-permute-start(bf16[3,48,1536]{2,1,0:T(8,128)(2,1)S(1)} %get-tuple-element.50.refs_6_.refs_13_), channel_id=1, source_target_pairs={{0,16},{1,113},{16,32},{17,1},{32,48},{33,17},{48,64},{49,33},{64,... | collective-permute-start | bytes 1327112 | tf_op jit(solution)/shard_map/second_z/ppermute | solution.py:49
  47.3 11.3 %copy-start = (bf16[1536,1024]{1,0:T(8,128)(2,1)S(1)}, bf16[1536,1024]{1,0:T(8,128)(2,1)}, u32[]{:S(2)}) copy-start(bf16[1536,1024]{1,0:T(8,128)(2,1)} %refs_22_.1) | copy-start | bytes 9437188
  51.1 7.4 %copy-start.3 = (f32[1,1536]{1,0:T(1,128)S(1)}, f32[1,1536]{1,0:T(1,128)}, u32[]{:S(2)}) copy-start(f32[1,1536]{1,0:T(1,128)} %refs_21_.1) | copy-start | bytes 18436
  51.2 7.4 %copy-start.4 = (f32[1024]{0:T(1024)S(1)}, f32[1024]{0:T(1024)}, u32[]{:S(2)}) copy-start(f32[1024]{0:T(1024)} %param.11) | copy-start | bytes 12292
  52.8 5.7 %collective-permute-start.17 = (bf16[3,96,1536]{2,1,0:T(8,128)(2,1)S(1)}, bf16[3,96,1536]{2,1,0:T(8,128)(2,1)S(1)}, u32[]{:S(2)}, u32[]{:S(2)}) collective-permute-start(bf16[3,96,1536]{2,1,0:T(8,128)(2,1)S(1)} %get-tuple-element.59.refs_2_.refs_17_), channel_id=1, source_target_pairs={{0,1},{1,0},{2,3},{3,2},{4,5},{5,4},{6,7},{7,6},{8,9},{9,8},{10,11... | collective-permute-start | bytes 2654216 | tf_op jit(solution)/shard_map/second_over_b/ppermute | solution.py:28
  54.6 4.0 %collective-permute-start.18 = (bf16[3,96,1536]{2,1,0:T(8,128)(2,1)S(1)}, bf16[3,96,1536]{2,1,0:T(8,128)(2,1)S(1)}, u32[]{:S(2)}, u32[]{:S(2)}) collective-permute-start(bf16[3,96,1536]{2,1,0:T(8,128)(2,1)S(1)} %get-tuple-element.60.refs_4_.refs_19_), channel_id=1, source_target_pairs={{0,1},{1,0},{2,3},{3,2},{4,5},{5,4},{6,7},{7,6},{8,9},{9,8},{10,11... | collective-permute-start | bytes 2654216 | tf_op jit(solution)/shard_map/distant_over_b/ppermute | solution.py:28
  54.7 3.9 %collective-permute-start.16 = (bf16[3,48,1536]{2,1,0:T(8,128)(2,1)S(1)}, bf16[3,48,1536]{2,1,0:T(8,128)(2,1)S(1)}, u32[]{:S(2)}, u32[]{:S(2)}) collective-permute-start(bf16[3,48,1536]{2,1,0:T(8,128)(2,1)S(1)} %get-tuple-element.58.refs_0_.refs_15_), channel_id=1, source_target_pairs={{0,1},{1,0},{2,3},{3,2},{4,5},{5,4},{6,7},{7,6},{8,9},{9,8},{10,11... | collective-permute-start | bytes 1327112 | tf_op jit(solution)/shard_map/second_z_b/ppermute | solution.py:28
  55.1 14.8 %collective-permute-start.20 = (bf16[144,1536]{1,0:T(8,128)(2,1)S(1)}, bf16[144,1536]{1,0:T(8,128)(2,1)S(1)}, u32[]{:S(2)}, u32[]{:S(2)}) collective-permute-start(bf16[144,1536]{1,0:T(8,128)(2,1)S(1)} %get-tuple-element.64), channel_id=1, source_target_pairs={{0,15},{1,14},{2,13},{3,12},{4,11},{5,10},{6,9},{7,8},{8,7},{9,6},... | collective-permute-start | bytes 1327112 | tf_op jit(solution)/shard_map/away/ppermute | solution.py:426
  62.5 18.1 %collective-permute-start.19 = (bf16[256,1024]{1,0:T(8,128)(2,1)S(1)}, bf16[256,1024]{1,0:T(8,128)(2,1)S(1)}, u32[]{:S(2)}, u32[]{:S(2)}) collective-permute-start(bf16[256,1024]{1,0:T(8,128)(2,1)S(1)} %finish.3), channel_id=1, source_target_pairs={{0,15},{1,14},{2,13},{3,12},{4,11},{5,10},{6,9},{7,8},{8,7},{9,6},... | collective-permute-start | bytes 1572872 | tf_op jit(solution)/shard_map/mirrored/ppermute | solution.py:437
where the time goes:
time: 82 us; the launch traced here: 81.8 us
  Pallas kernels  33.4 us (41%)
  starting transfers between devices  29.6 us (36%)
  waiting for transfers between devices  15.1 us (18%)
  local copies, waits for them, and re-layouts  2.21 us (3%)
  other arithmetic  1.22 us (1%)
    pallas_call x2, Pallas kernels, finish(): pl.pallas_call(functools.partial(finish_kernel, flipped, len(sources)), o...  9.62 us
    ppermute x4, starting transfers between devices, x_shift(): return lax.ppermute(value, ('x', 'core'), route)  9.44 us
    pallas_call x2, Pallas kernels, partial_sum(): pl.pallas_call(functools.partial(partial_kernel, len(sources), prev is No...  9.28 us
    ppermute x1, waiting for transfers between devices, per_device(): away = lax.ppermute(away, SEQ, mirror)  6.46 us
    ppermute x9, starting transfers between devices, core_swap(): return lax.ppermute(value, 'core', [(0, 1), (1, 0)])  6.15 us
    ppermute x1, starting transfers between devices, z_shift(): return lax.ppermute(value, ('z', 'core'), route)  5.33 us
    pallas_call x1, Pallas kernels, prepare(): pl.pallas_call(prepare_kernel, out_shape=stripes(rows + EDGE) + stripes(k...  5.01 us
    pallas_call x1, Pallas kernels, whole(): pl.pallas_call(functools.partial(whole_kernel, SOURCES), out_shape=jax.Sh...  4.94 us
  transfers between devices with their start and end apart: 21, of which 6 were waited for; matrix products, arithmetic and copies ran while one was open for 1% of the time, Pallas kernels for 40%

commit v1 on v0

--- a/solution.py
+++ b/solution.py
@@ -14,8 +14,8 @@
 VMEM_LIMIT = 24 * 1024 * 1024
 EDGE = 16
 TILE = 512
-PARTS = (12, 10, 10)
-SOURCES = (6, 6, 6)
+PARTS = (12, 8, 12)
+SOURCES = (6, 4, 8)
 PIECES = 32
 FIRST_HALF = 20
 ROWS = 128
@@ -73,6 +73,22 @@
     edge = lax.broadcasted_iota(jnp.int32, (EDGE, width), 0)
     tile = jnp.where(edge == 0, after, jnp.where(edge == EDGE - 1, before, 0.0))
     return tile.astype(jnp.bfloat16)
+
+
+def after_kernel(source_ref, token_ref, out_ref):
+    out_ref[...] = source_ref[...]
+
+
+def after(token, value):
+    inside = pl.BlockSpec(memory_space=pltpu.VMEM)
+    return pl.pallas_call(
+        after_kernel,
+        out_shape=jax.ShapeDtypeStruct(value.shape, value.dtype),
+        in_specs=[inside] * 2,
+        out_specs=inside,
+        compiler_params=pltpu.CompilerParams(vmem_limit_bytes=8 * 1024 * 1024),
+        name="after",
+    )(value, token)
 
 
 def halve_kernel(place_ref, shard_ref, out_ref):
@@ -260,7 +276,7 @@
 
 def predict(hidden_ref, head_ref, head_bias_ref, out_ref):
     rows = out_ref.shape[0]
-    @pl.loop(0, rows // ROWS)
+    @pl.loop(0, rows // ROWS, unroll=True)
     def _(block):
         here = pl.ds(pl.multiple_of(block * ROWS, ROWS), ROWS)
         logits = jnp.dot(hidden_ref[here, :], head_ref[...], preferred_element_type=jnp.float32)
@@ -272,7 +288,7 @@
 def finish_kernel(flipped, count, x_ref, *refs):
     sources, refs = refs[:count], refs[count:]
     prev_ref, bias_ref, head_ref, head_bias_ref, out_ref, hidden_ref = refs
-    @pl.loop(0, hidden_ref.shape[1] // TILE)
+    @pl.loop(0, hidden_ref.shape[1] // TILE, unroll=True)
     def _(tile):
         here = pl.ds(pl.multiple_of(tile * TILE, TILE), TILE)
         acc = convolve(x_ref[...], flipped, sources, here)
@@ -413,12 +429,12 @@
         near_over_b = core_swap(near_over)
     with jax.named_scope("distant_b"):
         distant_b = core_swap(distant)
+    shards_2 = [near_over, near_over_b, distant, distant_b]
+    acc, token = partial_sum(x_2, shards_2, acc)
     with jax.named_scope("second_b"):
-        second_b = core_swap(second)
-    shards_2 = [near_over, near_over_b, distant, distant_b, second, second_b]
-    acc, token = partial_sum(x_2, shards_2, acc)
-    second_over, distant_over, second_z, away = fence(
-        token, second_over, distant_over, second_z, away
+        second_b = core_swap(after(token, second))
+    second_over, distant_over, second_z, second_b, away = fence(
+        token, second_over, distant_over, second_z, second_b, away
     )
 
     mirror = [(i, ends - 1 - i) for i in range(ends)]
@@ -430,7 +446,7 @@
         distant_over_b = core_swap(distant_over)
     with jax.named_scope("second_z_b"):
         second_z_b = core_swap(second_z)
-    shards_3 = [second_z, second_z_b, second_over, second_over_b, distant_over, distant_over_b]
+    shards_3 = [second, second_b, second_z, second_z_b, second_over, second_over_b, distant_over, distant_over_b]
     rest = (conv_bias, head_weight, head_bias)
     reverse_tracks = finish(True, x_3[1], shards_3, acc[1], *rest)
     with jax.named_scope("mirrored"):

time: 82 us -> 80.9 us (0.987)
  waiting for transfers between devices: 15.1 us -> 11.6 us
  starting transfers between devices: 29.6 us -> 31.2 us
    ppermute x9, waiting for transfers between devices: 4.53 us -> 1.52 us  [core_swap(): return lax.ppermute(value, 'core', [(0, 1), (1, 0)])]
    ppermute x3, waiting for transfers between devices: 0.49 us -> 1.92 us  [y_shift(): return lax.ppermute(value, ('y_hi', 'y_lo', 'core'), route)]
    ppermute x1, starting transfers between devices: 0.61 us -> 1.94 us  [per_device(): away = lax.ppermute(away, SEQ, mirror)]
    ppermute x1, starting transfers between devices: 0.97 us -> 2.29 us  [per_device(): mirrored = lax.ppermute(reverse_tracks, SEQ, mirror)]
    ppermute x9, starting transfers between devices: 6.15 us -> 4.86 us  [core_swap(): return lax.ppermute(value, 'core', [(0, 1), (1, 0)])]
    ppermute x1, waiting for transfers between devices: 6.46 us -> 5.34 us  [per_device(): away = lax.ppermute(away, SEQ, mirror)]
  transfers between devices with their start and end apart: 21 -> 21, of which waited for: 6 -> 6; matrix products, arithmetic and copies ran while one was open for 1% -> 1% of each run, Pallas kernels for 40% -> 41%
where the time goes in v1:
time: 80.9 us; the launch traced here: 80.7 us
  Pallas kernels  34.2 us (42%)
  starting transfers between devices  31.2 us (39%)
  waiting for transfers between devices  11.6 us (14%)
  local copies, waits for them, and re-layouts  2.22 us (3%)
  other arithmetic  1.22 us (2%)
    ppermute x4, starting transfers between devices, x_shift(): return lax.ppermute(value, ('x', 'core'), route)  9.51 us
    pallas_call x2, Pallas kernels, finish(): pl.pallas_call(functools.partial(finish_kernel, flipped, len(sources)), o...  9.25 us
    pallas_call x2, Pallas kernels, partial_sum(): pl.pallas_call(functools.partial(partial_kernel, len(sources), prev is No...  9.19 us
    pallas_call x1, Pallas kernels, prepare(): pl.pallas_call(prepare_kernel, out_shape=stripes(rows + EDGE) + stripes(k...  5.69 us
    ppermute x1, starting transfers between devices, z_shift(): return lax.ppermute(value, ('z', 'core'), route)  5.52 us
    pallas_call x1, Pallas kernels, whole(): pl.pallas_call(functools.partial(whole_kernel, SOURCES), out_shape=jax.Sh...  5.43 us
    ppermute x1, waiting for transfers between devices, per_device(): away = lax.ppermute(away, SEQ, mirror)  5.34 us
    ppermute x9, starting transfers between devices, core_swap(): return lax.ppermute(value, 'core', [(0, 1), (1, 0)])  4.86 us
  transfers between devices with their start and end apart: 21, of which 6 were waited for; matrix products, arithmetic and copies ran while one was open for 1% of the time, Pallas kernels for 41%

profile of v1, /device:TPU:1, one launch (start us, length us, event | category | flops | bytes accessed | tf_op | source)
XLA Modules:
  0.0 80.7 jit_solution(6174696180291734796)
XLA Ops:
  0.0 3.3 %collective-permute-start = (bf16[3,96,1536]{2,1,0:T(8,128)(2,1)}, bf16[3,96,1536]{2,1,0:T(8,128)(2,1)S(1)}, u32[]{:S(2)}, u32[]{:S(2)}) collective-permute-start(bf16[3,96,1536]{2,1,0:T(8,128)(2,1)} %bitcast.34), channel_id=1, source_target_pairs={{0,4},{1,13},{4,8},{5,1},{8,12},{9,5},{12,0},{13,9},{2,6},{3,15},{... | collective-permute-start | bytes 2654216 | tf_op jit(solution)/shard_map/near/ppermute | solution.py:35
  3.3 2.7 %collective-permute-start.1 = (bf16[3,96,1536]{2,1,0:T(8,128)(2,1)}, bf16[3,96,1536]{2,1,0:T(8,128)(2,1)S(1)}, u32[]{:S(2)}, u32[]{:S(2)}) collective-permute-start(bf16[3,96,1536]{2,1,0:T(8,128)(2,1)} %bitcast.35), channel_id=1, source_target_pairs={{0,2},{1,131},{2,128},{3,1},{128,130},{129,3},{130,0},{131,129},{4... | collective-permute-start | bytes 2654216 | tf_op jit(solution)/shard_map/across/ppermute | solution.py:42
  6.0 0.8 %fusion = (bf16[1,1536]{1,0:T(2,128)(2,1)S(1)}, bf16[1,1536]{1,0:T(2,128)(2,1)S(1)}, bf16[1,1536]{1,0:T(2,128)(2,1)S(1)}, bf16[1,1536]{1,0:T(2,128)(2,1)S(1)}) fusion(bf16[384,1536]{1,0:T(8,128)(2,1)} %forward_ref.1, bf16[384,1536]{1,0:T(8,128)(2,1)} %reverse_ref.1), kind=kLoop, calls=%fused_computation.3 | loop fusion | bytes 24576 | tf_op jit(solution)/shard_map/high/slice | solution.py:404
  6.9 1.9 %collective-permute-start.2 = (bf16[2,1536]{1,0:T(2,128)(2,1)S(1)}, bf16[2,1536]{1,0:T(2,128)(2,1)S(1)}, u32[]{:S(2)}, u32[]{:S(2)}) collective-permute-start(bf16[2,1536]{1,0:T(2,128)(2,1)S(1)} %pad_maximum_fusion), channel_id=1, source_target_pairs={{0,1},{1,2},{2,3},{3,4},{4,5},{5,6},{6,7},{7,8},{8,9},{9,10},{10,1... | collective-permute-start | bytes 18440 | tf_op jit(solution)/shard_map/low/ppermute | solution.py:402
  8.8 2.4 %collective-permute-start.3 = (bf16[2,1536]{1,0:T(2,128)(2,1)S(1)}, bf16[2,1536]{1,0:T(2,128)(2,1)S(1)}, u32[]{:S(2)}, u32[]{:S(2)}) collective-permute-start(bf16[2,1536]{1,0:T(2,128)(2,1)S(1)} %pad_maximum_fusion.1), channel_id=1, source_target_pairs={{1,0},{2,1},{3,2},{4,3},{5,4},{6,5},{7,6},{8,7},{9,8},{10,9},{11,1... | collective-permute-start | bytes 18440 | tf_op jit(solution)/shard_map/high/ppermute | solution.py:404
  11.3 0.1 stack.137.place_ref
  11.4 0.0 copy-start.5
  11.5 1.3 %copy-done.5 = bf16[384,1536]{1,0:T(8,128)(2,1)S(1)} copy-done((bf16[384,1536]{1,0:T(8,128)(2,1)S(1)}, bf16[384,1536]{1,0:T(8,128)(2,1)}, u32[]{:S(2)}) %copy-start.5) | copy-done | bytes 1179672
  12.7 3.1 %order.1 = (bf16[1536,576]{1,0:T(8,128)(2,1)S(1)}, bf16[1536,384]{1,0:T(8,128)(2,1)S(1)}, bf16[1536,576]{1,0:T(8,128)(2,1)S(1)}, bf16[384,1536]{1,0:T(8,128)(2,1)S(1)}, f32[8,128]{1,0:T(8,128)S(1)}) custom-call(s32[32]{0:T(128)S(1)} %stack.137.place_ref, bf16[384,1536]{1,0:T(8,128)(2,1)S(1)} %copy-done.5), custom_call_target="tpu_custom_call" | custom-call | flops 14495514624 | bytes 4718592 | tf_op jit(solution)/shard_map/order/pallas_call | solution.py:147
  15.8 0.0 copy-start.1
  15.8 0.0 collective-permute-done.2.refs_2_
  15.8 0.0 collective-permute-done.3.refs_3_
  15.8 0.5 collective-permute-done.1.refs_1_
  16.3 0.2 fence.3
  16.6 1.4 %collective-permute-start.6 = (bf16[3,96,1536]{2,1,0:T(8,128)(2,1)S(1)}, bf16[3,96,1536]{2,1,0:T(8,128)(2,1)S(1)}, u32[]{:S(2)}, u32[]{:S(2)}) collective-permute-start(bf16[3,96,1536]{2,1,0:T(8,128)(2,1)S(1)} %get-tuple-element.45.refs_4_.refs_5_), channel_id=1, source_target_pairs={{0,1},{1,0},{2,3},{3,2},{4,5},{5,4},{6,7},{7,6},{8,9},{9,8},{10,11... | collective-permute-start | bytes 2654216 | tf_op jit(solution)/shard_map/across_b/ppermute | solution.py:28
  18.0 0.1 collective-permute-start.9
  18.1 3.0 %collective-permute-start.4 = (bf16[3,96,1536]{2,1,0:T(8,128)(2,1)S(1)}, bf16[3,96,1536]{2,1,0:T(8,128)(2,1)S(1)}, u32[]{:S(2)}, u32[]{:S(2)}) collective-permute-start(bf16[3,96,1536]{2,1,0:T(8,128)(2,1)S(1)} %get-tuple-element.44.refs_6_.refs_7_), channel_id=1, source_target_pairs={{0,4},{1,13},{4,8},{5,1},{8,12},{9,5},{12,0},{13,9},{2,6},{3,15},{... | collective-permute-start | bytes 2654216 | tf_op jit(solution)/shard_map/distant/ppermute | solution.py:35
  21.1 0.6 halve.1
  21.7 1.4 %collective-permute-start.8 = (bf16[3,48,1536]{2,1,0:T(8,128)(2,1)S(1)}, bf16[3,48,1536]{2,1,0:T(8,128)(2,1)S(1)}, u32[]{:S(2)}, u32[]{:S(2)}) collective-permute-start(bf16[3,48,1536]{2,1,0:T(8,128)(2,1)S(1)} %halve.1), channel_id=1, source_target_pairs={{0,4},{1,13},{4,8},{5,1},{8,12},{9,5},{12,0},{13,9},{2,6},{3,15},{... | collective-permute-start | bytes 1327112 | tf_op jit(solution)/shard_map/second/ppermute | solution.py:35
  23.1 5.7 %prepare.1 = (bf16[400,576]{1,0:T(8,128)(2,1)S(1)}, bf16[400,384]{1,0:T(8,128)(2,1)S(1)}, bf16[400,576]{1,0:T(8,128)(2,1)S(1)}, bf16[272,576]{1,0:T(8,128)(2,1)S...) custom-call(bf16[384,1536]{1,0:T(8,128)(2,1)S(1)} %copy-done.1, ...), custom_call_target="tpu_custom_call" | custom-call | flops 1000 | bytes 1000 | tf_op jit(solution)/shard_map/prepare/pallas_call | solution.py:206
  28.8 0.0 collective-permute-done.6.refs_5_.refs_2_
  28.8 0.0 collective-permute-done.9.refs_7_.refs_8_
  28.8 5.3 %partial_sum.2 = (f32[384,1536]{1,0:T(8,128)S(1)}, f32[256,1536]{1,0:T(8,128)S(1)}, f32[8,128]{1,0:T(8,128)S(1)}) custom-call(bf16[400,576]{1,0:T(8,128)(2,1)S(1)} %get-tuple-element.46.refs_0_, bf16[272,576]{1,0:T(8,128)(2,1)S(1)} %get-tuple-element.47.refs_1_, bf16[3,96,1536]{2,1,0:T(8,128)(2,1)S(1)} %bitcast.37, ...), custom_call_target="tpu_custom_call" | custom-call | flops 3397386240 | bytes 5308416 | tf_op jit(solution)/shard_map/partial_sum/pallas_call | solution.py:255
  34.1 1.6 %collective-permute-done.8.refs_3_ = bf16[3,48,1536]{2,1,0:T(8,128)(2,1)S(1)} collective-permute-done((bf16[3,48,1536]{2,1,0:T(8,128)(2,1)S(1)}, bf16[3,48,1536]{2,1,0:T(8,128)(2,1)S(1)}, u32[]{:S(2)}, u32[]{:S(2)}) %collective-permute-start.8) | collective-permute-done | bytes 442400 | tf_op jit(solution)/shard_map/second/ppermute | solution.py:35
  35.8 0.4 fence.4
  36.2 1.8 %collective-permute-start.13 = (bf16[3,96,1536]{2,1,0:T(8,128)(2,1)S(1)}, bf16[3,96,1536]{2,1,0:T(8,128)(2,1)S(1)}, u32[]{:S(2)}, u32[]{:S(2)}) collective-permute-start(bf16[3,96,1536]{2,1,0:T(8,128)(2,1)S(1)} %get-tuple-element.54.refs_2_.refs_9_), channel_id=1, source_target_pairs={{0,1},{1,0},{2,3},{3,2},{4,5},{5,4},{6,7},{7,6},{8,9},{9,8},{10,11... | collective-permute-start | bytes 2654216 | tf_op jit(solution)/shard_map/near_over_b/ppermute | solution.py:28
  38.0 0.1 collective-permute-start.14
  38.1 1.8 %collective-permute-start.10 = (bf16[3,96,1536]{2,1,0:T(8,128)(2,1)S(1)}, bf16[3,96,1536]{2,1,0:T(8,128)(2,1)S(1)}, u32[]{:S(2)}, u32[]{:S(2)}) collective-permute-start(bf16[3,96,1536]{2,1,0:T(8,128)(2,1)S(1)} %get-tuple-element.50.refs_6_), channel_id=1, source_target_pairs={{0,4},{1,13},{4,8},{5,1},{8,12},{9,5},{12,0},{13,9},{2,6},{3,15},{... | collective-permute-start | bytes 2654216 | tf_op jit(solution)/shard_map/second_over/ppermute | solution.py:35
  39.9 5.5 %collective-permute-start.12 = (bf16[3,48,1536]{2,1,0:T(8,128)(2,1)S(1)}, bf16[3,48,1536]{2,1,0:T(8,128)(2,1)S(1)}, u32[]{:S(2)}, u32[]{:S(2)}) collective-permute-start(bf16[3,48,1536]{2,1,0:T(8,128)(2,1)S(1)} %get-tuple-element.49.source_ref.refs_0_.refs_13_), channel_id=1, source_target_pairs={{0,16},{1,113},{16,32},{17,1},{32,48},{33,17},{48,64},{49,33},{64,... | collective-permute-start | bytes 1327112 | tf_op jit(solution)/shard_map/second_z/ppermute | solution.py:49
  45.4 3.9 %partial_sum.3 = (f32[384,1536]{1,0:T(8,128)S(1)}, f32[256,1536]{1,0:T(8,128)S(1)}, f32[8,128]{1,0:T(8,128)S(1)}) custom-call(bf16[400,384]{1,0:T(8,128)(2,1)S(1)} %get-tuple-element.52.refs_0_, bf16[272,384]{1,0:T(8,128)(2,1)S(1)} %get-tuple-element.53.refs_1_, ...), custom_call_target="tpu_custom_call", output_to_operand_aliasing={{0}: (6, {}), {1}: (7, {})} | custom-call | flops 2264924160 | bytes 3538944 | tf_op jit(solution)/shard_map/partial_sum/pallas_call | solution.py:255
  49.3 0.0 copy-start
  49.3 0.0 copy-start.3
  49.4 0.0 copy-start.4
  49.4 0.1 collective-permute-start.15
  49.5 1.2 %collective-permute-done.12.refs_2_ = bf16[3,48,1536]{2,1,0:T(8,128)(2,1)S(1)} collective-permute-done((bf16[3,48,1536]{2,1,0:T(8,128)(2,1)S(1)}, bf16[3,48,1536]{2,1,0:T(8,128)(2,1)S(1)}, u32[]{:S(2)}, u32[]{:S(2)}) %collective-permute-start.12) | collective-permute-done | bytes 442400 | tf_op jit(solution)/shard_map/second_z/ppermute | solution.py:49
  50.7 1.4 %collective-permute-done.11.refs_1_ = bf16[3,96,1536]{2,1,0:T(8,128)(2,1)S(1)} collective-permute-done((bf16[3,96,1536]{2,1,0:T(8,128)(2,1)S(1)}, bf16[3,96,1536]{2,1,0:T(8,128)(2,1)S(1)}, u32[]{:S(2)}, u32[]{:S(2)}) %collective-permute-start.11) | collective-permute-done | bytes 884768 | tf_op jit(solution)/shard_map/distant_over/ppermute | solution.py:42
  52.1 0.4 fence.5
  52.4 0.8 collective-permute-start.17
  53.2 0.1 collective-permute-start.18
  53.3 0.4 collective-permute-start.16
  53.7 1.9 %collective-permute-start.20 = (bf16[144,1536]{1,0:T(8,128)(2,1)S(1)}, bf16[144,1536]{1,0:T(8,128)(2,1)S(1)}, u32[]{:S(2)}, u32[]{:S(2)}) collective-permute-start(bf16[144,1536]{1,0:T(8,128)(2,1)S(1)} %get-tuple-element.66), channel_id=1, source_target_pairs={{0,15},{1,14},{2,13},{3,12},{4,11},{5,10},{6,9},{7,8},{8,7},{9,6},... | collective-permute-start | bytes 1327112 | tf_op jit(solution)/shard_map/away/ppermute | solution.py:442
  55.7 1.5 %collective-permute-done.16.refs_3_.refs_16_ = bf16[3,48,1536]{2,1,0:T(8,128)(2,1)S(1)} collective-permute-done((bf16[3,48,1536]{2,1,0:T(8,128)(2,1)S(1)}, bf16[3,48,1536]{2,1,0:T(8,128)(2,1)S(1)}, u32[]{:S(2)}, u32[]{:S(2)}) %collective-permute-start.16) | collective-permute-done | bytes 442400 | tf_op jit(solution)/shard_map/second_z_b/ppermute | solution.py:28
  57.2 3.7 %finish.3 = bf16[256,1024]{1,0:T(8,128)(2,1)S(1)} custom-call(bf16[272,576]{1,0:T(8,128)(2,1)S(1)} %get-tuple-element.64.x_ref, bf16[3,48,1536]{2,1,0:T(8,128)(2,1)S(1)} %get-tuple-element.49.source_ref.refs_0_.refs_13_, bf16[3,48,1536]{2,1,0:T(8,128)(2,1)S(1)} %get-tuple-element.59.refs_1_.refs_14_, ...), custom_call_target="tpu_custom_call" | custom-call | flops 2164260864 | bytes 8454144 | tf_op jit(solution)/shard_map/finish/pallas_call | solution.py:304
  60.9 2.3 %collective-permute-start.19 = (bf16[256,1024]{1,0:T(8,128)(2,1)S(1)}, bf16[256,1024]{1,0:T(8,128)(2,1)S(1)}, u32[]{:S(2)}, u32[]{:S(2)}) collective-permute-start(bf16[256,1024]{1,0:T(8,128)(2,1)S(1)} %finish.3), channel_id=1, source_target_pairs={{0,15},{1,14},{2,13},{3,12},{4,11},{5,10},{6,9},{7,8},{8,7},{9,6},... | collective-permute-start | bytes 1572872 | tf_op jit(solution)/shard_map/mirrored/ppermute | solution.py:453
  63.2 5.3 %collective-permute-done.20.away_ref = bf16[144,1536]{1,0:T(8,128)(2,1)S(1)} collective-permute-done((bf16[144,1536]{1,0:T(8,128)(2,1)S(1)}, bf16[144,1536]{1,0:T(8,128)(2,1)S(1)}, u32[]{:S(2)}, u32[]{:S(2)}) %collective-permute-start.20) | collective-permute-done | bytes 442400 | tf_op jit(solution)/shard_map/away/ppermute | solution.py:442
  68.6 5.4 %whole.1 = bf16[128,1024]{1,0:T(8,128)(2,1)S(1)} custom-call(bf16[144,1536]{1,0:T(8,128)(2,1)S(1)} %collective-permute-done.20.away_ref, bf16[1536,576]{1,0:T(8,128)(2,1)S(1)} %get-tuple-element.40.refs_0_, bf16[1536,384]{1,0:T(8,128)(2,1)S(1)} %get-tuple-element.41.refs_1_, bf16[1536,576]{1,0:T(8,128)(2,1)S(1)} %get-tuple-element.42.refs_2_, ...), custom_call_target="tpu_custom_call" | custom-call | flops 2818572288 | bytes 14155776 | tf_op jit(solution)/shard_map/whole/pallas_call | solution.py:344
  74.0 5.5 %finish.2 = bf16[384,1024]{1,0:T(8,128)(2,1)S(1)} custom-call(bf16[400,576]{1,0:T(8,128)(2,1)S(1)} %get-tuple-element.43.x_ref, bf16[3,48,1536]{2,1,0:T(8,128)(2,1)S(1)} %get-tuple-element.49.source_ref.refs_0_.refs_13_, bf16[3,48,1536]{2,1,0:T(8,128)(2,1)S(1)} %get-tuple-element.59.refs_1_.refs_14_, ...), custom_call_target="tpu_custom_call" | custom-call | flops 3246391296 | bytes 8454144 | tf_op jit(solution)/shard_map/finish/pallas_call | solution.py:304
  79.5 1.2 %multiply_convert_fusion = bf16[384,1024]{1,0:T(8,128)(2,1)} fusion(bf16[384,1024]{1,0:T(8,128)(2,1)S(1)} %finish.2, bf16[128,1024]{1,0:T(8,128)(2,1)S(1)} %whole.1, bf16[256,1024]{1,0:T(8,128)(2,1)S(1)} %collective-permute-done.19), kind=kLoop, calls=%fused_computation | loop fusion | flops 3145728 | bytes 2359296 | tf_op jit(solution)/shard_map/convert_element_type | solution.py:458
  (23 shorter events, 0.1 us)
Async XLA Ops:
  0.0 15.8 %collective-permute-start = (bf16[3,96,1536]{2,1,0:T(8,128)(2,1)}, bf16[3,96,1536]{2,1,0:T(8,128)(2,1)S(1)}, u32[]{:S(2)}, u32[]{:S(2)}) collective-permute-start(bf16[3,96,1536]{2,1,0:T(8,128)(2,1)} %bitcast.34), channel_id=1, source_target_pairs={{0,4},{1,13},{4,8},{5,1},{8,12},{9,5},{12,0},{13,9},{2,6},{3,15},{... | collective-permute-start | bytes 2654216 | tf_op jit(solution)/shard_map/near/ppermute | solution.py:35
  3.3 13.0 %collective-permute-start.1 = (bf16[3,96,1536]{2,1,0:T(8,128)(2,1)}, bf16[3,96,1536]{2,1,0:T(8,128)(2,1)S(1)}, u32[]{:S(2)}, u32[]{:S(2)}) collective-permute-start(bf16[3,96,1536]{2,1,0:T(8,128)(2,1)} %bitcast.35), channel_id=1, source_target_pairs={{0,2},{1,131},{2,128},{3,1},{128,130},{129,3},{130,0},{131,129},{4... | collective-permute-start | bytes 2654216 | tf_op jit(solution)/shard_map/across/ppermute | solution.py:42
  6.0 15.0 %collective-permute-start.7 = (bf16[3,96,1536]{2,1,0:T(8,128)(2,1)}, bf16[3,96,1536]{2,1,0:T(8,128)(2,1)S(1)}, u32[]{:S(2)}, u32[]{:S(2)}) collective-permute-start(bf16[3,96,1536]{2,1,0:T(8,128)(2,1)} %bitcast.36), channel_id=1, source_target_pairs={{0,1},{1,0},{2,3},{3,2},{4,5},{5,4},{6,7},{7,6},{8,9},{9,8},{10,11... | collective-permute-start | bytes 2654216 | tf_op jit(solution)/shard_map/sibling/ppermute | solution.py:28
  6.9 8.9 %collective-permute-start.2 = (bf16[2,1536]{1,0:T(2,128)(2,1)S(1)}, bf16[2,1536]{1,0:T(2,128)(2,1)S(1)}, u32[]{:S(2)}, u32[]{:S(2)}) collective-permute-start(bf16[2,1536]{1,0:T(2,128)(2,1)S(1)} %pad_maximum_fusion), channel_id=1, source_target_pairs={{0,1},{1,2},{2,3},{3,4},{4,5},{5,6},{6,7},{7,8},{8,9},{9,10},{10,1... | collective-permute-start | bytes 18440 | tf_op jit(solution)/shard_map/low/ppermute | solution.py:402
  8.8 7.0 %collective-permute-start.3 = (bf16[2,1536]{1,0:T(2,128)(2,1)S(1)}, bf16[2,1536]{1,0:T(2,128)(2,1)S(1)}, u32[]{:S(2)}, u32[]{:S(2)}) collective-permute-start(bf16[2,1536]{1,0:T(2,128)(2,1)S(1)} %pad_maximum_fusion.1), channel_id=1, source_target_pairs={{1,0},{2,1},{3,2},{4,3},{5,4},{6,5},{7,6},{8,7},{9,8},{10,9},{11,1... | collective-permute-start | bytes 18440 | tf_op jit(solution)/shard_map/high/ppermute | solution.py:404
  11.4 1.3 %copy-start.5 = (bf16[384,1536]{1,0:T(8,128)(2,1)S(1)}, bf16[384,1536]{1,0:T(8,128)(2,1)}, u32[]{:S(2)}) copy-start(bf16[384,1536]{1,0:T(8,128)(2,1)} %reverse_ref.1) | copy-start | bytes 3538948
  15.8 7.3 %copy-start.1 = (bf16[384,1536]{1,0:T(8,128)(2,1)S(1)}, bf16[384,1536]{1,0:T(8,128)(2,1)}, u32[]{:S(2)}) copy-start(bf16[384,1536]{1,0:T(8,128)(2,1)} %forward_ref.1) | copy-start | bytes 3538948
  16.6 12.2 %collective-permute-start.6 = (bf16[3,96,1536]{2,1,0:T(8,128)(2,1)S(1)}, bf16[3,96,1536]{2,1,0:T(8,128)(2,1)S(1)}, u32[]{:S(2)}, u32[]{:S(2)}) collective-permute-start(bf16[3,96,1536]{2,1,0:T(8,128)(2,1)S(1)} %get-tuple-element.45.refs_4_.refs_5_), channel_id=1, source_target_pairs={{0,1},{1,0},{2,3},{3,2},{4,5},{5,4},{6,7},{7,6},{8,9},{9,8},{10,11... | collective-permute-start | bytes 2654216 | tf_op jit(solution)/shard_map/across_b/ppermute | solution.py:28
  18.0 10.8 %collective-permute-start.9 = (bf16[3,96,1536]{2,1,0:T(8,128)(2,1)S(1)}, bf16[3,96,1536]{2,1,0:T(8,128)(2,1)S(1)}, u32[]{:S(2)}, u32[]{:S(2)}) collective-permute-start(bf16[3,96,1536]{2,1,0:T(8,128)(2,1)S(1)} %get-tuple-element.44.refs_6_.refs_7_), channel_id=1, source_target_pairs={{0,1},{1,0},{2,3},{3,2},{4,5},{5,4},{6,7},{7,6},{8,9},{9,8},{10,11... | collective-permute-start | bytes 2654216 | tf_op jit(solution)/shard_map/near_b/ppermute | solution.py:28
  18.1 17.7 %collective-permute-start.4 = (bf16[3,96,1536]{2,1,0:T(8,128)(2,1)S(1)}, bf16[3,96,1536]{2,1,0:T(8,128)(2,1)S(1)}, u32[]{:S(2)}, u32[]{:S(2)}) collective-permute-start(bf16[3,96,1536]{2,1,0:T(8,128)(2,1)S(1)} %get-tuple-element.44.refs_6_.refs_7_), channel_id=1, source_target_pairs={{0,4},{1,13},{4,8},{5,1},{8,12},{9,5},{12,0},{13,9},{2,6},{3,15},{... | collective-permute-start | bytes 2654216 | tf_op jit(solution)/shard_map/distant/ppermute | solution.py:35
  21.1 14.7 %collective-permute-start.5 = (bf16[3,96,1536]{2,1,0:T(8,128)(2,1)S(1)}, bf16[3,96,1536]{2,1,0:T(8,128)(2,1)S(1)}, u32[]{:S(2)}, u32[]{:S(2)}) collective-permute-start(bf16[3,96,1536]{2,1,0:T(8,128)(2,1)S(1)} %get-tuple-element.44.refs_6_.refs_7_), channel_id=1, source_target_pairs={{0,2},{1,131},{2,128},{3,1},{128,130},{129,3},{130,0},{131,129},{4... | collective-permute-start | bytes 2654216 | tf_op jit(solution)/shard_map/near_over/ppermute | solution.py:42
  21.7 14.1 %collective-permute-start.8 = (bf16[3,48,1536]{2,1,0:T(8,128)(2,1)S(1)}, bf16[3,48,1536]{2,1,0:T(8,128)(2,1)S(1)}, u32[]{:S(2)}, u32[]{:S(2)}) collective-permute-start(bf16[3,48,1536]{2,1,0:T(8,128)(2,1)S(1)} %halve.1), channel_id=1, source_target_pairs={{0,4},{1,13},{4,8},{5,1},{8,12},{9,5},{12,0},{13,9},{2,6},{3,15},{... | collective-permute-start | bytes 1327112 | tf_op jit(solution)/shard_map/second/ppermute | solution.py:35
  23.1 5.7 %copy-start.2 = (bf16[1,3,96,1536]{3,2,1,0:T(8,128)(2,1)S(1)}, bf16[1,3,96,1536]{3,2,1,0:T(8,128)(2,1)}, u32[]{:S(2)}) copy-start(bf16[1,3,96,1536]{3,2,1,0:T(8,128)(2,1)} %param.8) | copy-start | bytes 2654212
  36.2 9.2 %collective-permute-start.13 = (bf16[3,96,1536]{2,1,0:T(8,128)(2,1)S(1)}, bf16[3,96,1536]{2,1,0:T(8,128)(2,1)S(1)}, u32[]{:S(2)}, u32[]{:S(2)}) collective-permute-start(bf16[3,96,1536]{2,1,0:T(8,128)(2,1)S(1)} %get-tuple-element.54.refs_2_.refs_9_), channel_id=1, source_target_pairs={{0,1},{1,0},{2,3},{3,2},{4,5},{5,4},{6,7},{7,6},{8,9},{9,8},{10,11... | collective-permute-start | bytes 2654216 | tf_op jit(solution)/shard_map/near_over_b/ppermute | solution.py:28
  38.0 7.4 %collective-permute-start.14 = (bf16[3,96,1536]{2,1,0:T(8,128)(2,1)S(1)}, bf16[3,96,1536]{2,1,0:T(8,128)(2,1)S(1)}, u32[]{:S(2)}, u32[]{:S(2)}) collective-permute-start(bf16[3,96,1536]{2,1,0:T(8,128)(2,1)S(1)} %get-tuple-element.51.refs_4_.refs_11_), channel_id=1, source_target_pairs={{0,1},{1,0},{2,3},{3,2},{4,5},{5,4},{6,7},{7,6},{8,9},{9,8},{10,11... | collective-permute-start | bytes 2654216 | tf_op jit(solution)/shard_map/distant_b/ppermute | solution.py:28
  38.1 12.6 %collective-permute-start.10 = (bf16[3,96,1536]{2,1,0:T(8,128)(2,1)S(1)}, bf16[3,96,1536]{2,1,0:T(8,128)(2,1)S(1)}, u32[]{:S(2)}, u32[]{:S(2)}) collective-permute-start(bf16[3,96,1536]{2,1,0:T(8,128)(2,1)S(1)} %get-tuple-element.50.refs_6_), channel_id=1, source_target_pairs={{0,4},{1,13},{4,8},{5,1},{8,12},{9,5},{12,0},{13,9},{2,6},{3,15},{... | collective-permute-start | bytes 2654216 | tf_op jit(solution)/shard_map/second_over/ppermute | solution.py:35
  39.9 12.2 %collective-permute-start.11 = (bf16[3,96,1536]{2,1,0:T(8,128)(2,1)S(1)}, bf16[3,96,1536]{2,1,0:T(8,128)(2,1)S(1)}, u32[]{:S(2)}, u32[]{:S(2)}) collective-permute-start(bf16[3,96,1536]{2,1,0:T(8,128)(2,1)S(1)} %get-tuple-element.51.refs_4_.refs_11_), channel_id=1, source_target_pairs={{0,2},{1,131},{2,128},{3,1},{128,130},{129,3},{130,0},{131,129},{4... | collective-permute-start | bytes 2654216 | tf_op jit(solution)/shard_map/distant_over/ppermute | solution.py:42
  39.9 10.8 %collective-permute-start.12 = (bf16[3,48,1536]{2,1,0:T(8,128)(2,1)S(1)}, bf16[3,48,1536]{2,1,0:T(8,128)(2,1)S(1)}, u32[]{:S(2)}, u32[]{:S(2)}) collective-permute-start(bf16[3,48,1536]{2,1,0:T(8,128)(2,1)S(1)} %get-tuple-element.49.source_ref.refs_0_.refs_13_), channel_id=1, source_target_pairs={{0,16},{1,113},{16,32},{17,1},{32,48},{33,17},{48,64},{49,33},{64,... | collective-permute-start | bytes 1327112 | tf_op jit(solution)/shard_map/second_z/ppermute | solution.py:49
  49.3 7.9 %copy-start = (bf16[1536,1024]{1,0:T(8,128)(2,1)S(1)}, bf16[1536,1024]{1,0:T(8,128)(2,1)}, u32[]{:S(2)}) copy-start(bf16[1536,1024]{1,0:T(8,128)(2,1)} %refs_22_.1) | copy-start | bytes 9437188
  49.3 7.8 %copy-start.3 = (f32[1,1536]{1,0:T(1,128)S(1)}, f32[1,1536]{1,0:T(1,128)}, u32[]{:S(2)}) copy-start(f32[1,1536]{1,0:T(1,128)} %refs_21_.1) | copy-start | bytes 18436
  49.4 7.8 %copy-start.4 = (f32[1024]{0:T(1024)S(1)}, f32[1024]{0:T(1024)}, u32[]{:S(2)}) copy-start(f32[1024]{0:T(1024)} %param.11) | copy-start | bytes 12292
  49.4 2.7 %collective-permute-start.15 = (bf16[3,48,1536]{2,1,0:T(8,128)(2,1)S(1)}, bf16[3,48,1536]{2,1,0:T(8,128)(2,1)S(1)}, u32[]{:S(2)}, u32[]{:S(2)}) collective-permute-start(bf16[3,48,1536]{2,1,0:T(8,128)(2,1)S(1)} %after.1), channel_id=1, source_target_pairs={{0,1},{1,0},{2,3},{3,2},{4,5},{5,4},{6,7},{7,6},{8,9},{9,8},{10,11... | collective-permute-start | bytes 1327112 | tf_op jit(solution)/shard_map/second_b/ppermute | solution.py:28
  52.4 4.7 %collective-permute-start.17 = (bf16[3,96,1536]{2,1,0:T(8,128)(2,1)S(1)}, bf16[3,96,1536]{2,1,0:T(8,128)(2,1)S(1)}, u32[]{:S(2)}, u32[]{:S(2)}) collective-permute-start(bf16[3,96,1536]{2,1,0:T(8,128)(2,1)S(1)} %get-tuple-element.61.refs_4_.refs_17_), channel_id=1, source_target_pairs={{0,1},{1,0},{2,3},{3,2},{4,5},{5,4},{6,7},{7,6},{8,9},{9,8},{10,11... | collective-permute-start | bytes 2654216 | tf_op jit(solution)/shard_map/second_over_b/ppermute | solution.py:28
  53.2 4.0 %collective-permute-start.18 = (bf16[3,96,1536]{2,1,0:T(8,128)(2,1)S(1)}, bf16[3,96,1536]{2,1,0:T(8,128)(2,1)S(1)}, u32[]{:S(2)}, u32[]{:S(2)}) collective-permute-start(bf16[3,96,1536]{2,1,0:T(8,128)(2,1)S(1)} %get-tuple-element.62.refs_6_.refs_19_), channel_id=1, source_target_pairs={{0,1},{1,0},{2,3},{3,2},{4,5},{5,4},{6,7},{7,6},{8,9},{9,8},{10,11... | collective-permute-start | bytes 2654216 | tf_op jit(solution)/shard_map/distant_over_b/ppermute | solution.py:28
  53.3 3.9 %collective-permute-start.16 = (bf16[3,48,1536]{2,1,0:T(8,128)(2,1)S(1)}, bf16[3,48,1536]{2,1,0:T(8,128)(2,1)S(1)}, u32[]{:S(2)}, u32[]{:S(2)}) collective-permute-start(bf16[3,48,1536]{2,1,0:T(8,128)(2,1)S(1)} %get-tuple-element.60.refs_2_.refs_15_), channel_id=1, source_target_pairs={{0,1},{1,0},{2,3},{3,2},{4,5},{5,4},{6,7},{7,6},{8,9},{9,8},{10,11... | collective-permute-start | bytes 1327112 | tf_op jit(solution)/shard_map/second_z_b/ppermute | solution.py:28
  53.7 14.8 %collective-permute-start.20 = (bf16[144,1536]{1,0:T(8,128)(2,1)S(1)}, bf16[144,1536]{1,0:T(8,128)(2,1)S(1)}, u32[]{:S(2)}, u32[]{:S(2)}) collective-permute-start(bf16[144,1536]{1,0:T(8,128)(2,1)S(1)} %get-tuple-element.66), channel_id=1, source_target_pairs={{0,15},{1,14},{2,13},{3,12},{4,11},{5,10},{6,9},{7,8},{8,7},{9,6},... | collective-permute-start | bytes 1327112 | tf_op jit(solution)/shard_map/away/ppermute | solution.py:442
  60.9 18.6 %collective-permute-start.19 = (bf16[256,1024]{1,0:T(8,128)(2,1)S(1)}, bf16[256,1024]{1,0:T(8,128)(2,1)S(1)}, u32[]{:S(2)}, u32[]{:S(2)}) collective-permute-start(bf16[256,1024]{1,0:T(8,128)(2,1)S(1)} %finish.3), channel_id=1, source_target_pairs={{0,15},{1,14},{2,13},{3,12},{4,11},{5,10},{6,9},{7,8},{8,7},{9,6},... | collective-permute-start | bytes 1572872 | tf_op jit(solution)/shard_map/mirrored/ppermute | solution.py:453

commit v2 on v1

--- a/solution.py
+++ b/solution.py
@@ -317,7 +317,7 @@
     )(x, *sources, prev, bias, head, head_bias[None])
 
 
-def whole_kernel(sizes, away_ref, *refs):
+def whole_kernel(sizes, forward_ref, away_ref, *refs):
     moves, refs = refs[: len(sizes)], refs[len(sizes) :]
     sources, refs = refs[: sum(sizes)], refs[sum(sizes) :]
     bias_ref, head_ref, head_bias_ref, out_ref, hidden_ref = refs
@@ -337,14 +337,14 @@
     predict(hidden_ref, head_ref, head_bias_ref, out_ref)
 
 
-def whole(away, moves, sources, bias, head, head_bias):
+def whole(forward_tracks, away, moves, sources, bias, head, head_bias):
     rows = away.shape[0] - EDGE
     channels, tracks = head.shape
     inside = pl.BlockSpec(memory_space=pltpu.VMEM)
     return pl.pallas_call(
         functools.partial(whole_kernel, SOURCES),
         out_shape=jax.ShapeDtypeStruct((rows, tracks), jnp.bfloat16),
-        in_specs=[inside] * (len(moves) + len(sources) + 4),
+        in_specs=[inside] * (len(moves) + len(sources) + 5),
         out_specs=inside,
         scratch_shapes=[pltpu.VMEM((rows, channels), jnp.bfloat16)],
         compiler_params=pltpu.CompilerParams(vmem_limit_bytes=VMEM_LIMIT),
@@ -354,7 +354,7 @@
             transcendentals=rows * channels,
         ),
         name="whole",
-    )(away, *moves, *sources, bias, head, head_bias[None])
+    )(forward_tracks, away, *moves, *sources, bias, head, head_bias[None])
 
 
 def per_device(forward_embed, reverse_embed, conv_weight, conv_bias, head_weight, head_bias):
@@ -433,8 +433,10 @@
     acc, token = partial_sum(x_2, shards_2, acc)
     with jax.named_scope("second_b"):
         second_b = core_swap(after(token, second))
-    second_over, distant_over, second_z, second_b, away = fence(
-        token, second_over, distant_over, second_z, second_b, away
+    with jax.named_scope("second_z_b"):
+        second_z_b = core_swap(after(token, second_z))
+    second_over, distant_over, second_z_b, second_b, away = fence(
+        token, second_over, distant_over, second_z_b, second_b, away
     )
 
     mirror = [(i, ends - 1 - i) for i in range(ends)]
@@ -444,15 +446,13 @@
         second_over_b = core_swap(second_over)
     with jax.named_scope("distant_over_b"):
         distant_over_b = core_swap(distant_over)
-    with jax.named_scope("second_z_b"):
-        second_z_b = core_swap(second_z)
     shards_3 = [second, second_b, second_z, second_z_b, second_over, second_over_b, distant_over, distant_over_b]
     rest = (conv_bias, head_weight, head_bias)
     reverse_tracks = finish(True, x_3[1], shards_3, acc[1], *rest)
     with jax.named_scope("mirrored"):
         mirrored = lax.ppermute(reverse_tracks, SEQ, mirror)
     forward_tracks = finish(False, x_3[0], shards_3, acc[0], *rest)
-    away_tracks = whole(away, moves, shards_1 + shards_2 + shards_3, *rest)
+    away_tracks = whole(forward_tracks, away, moves, shards_1 + shards_2 + shards_3, *rest)
     reverse = jnp.concatenate([mirrored, away_tracks])
     mean = 0.5 * (forward_tracks.astype(jnp.float32) + reverse.astype(jnp.float32))
     return mean.astype(jnp.bfloat16)

time: 80.9 us -> 85.6 us (1.058)
  waiting for transfers between devices: 11.6 us -> 17.5 us
  starting transfers between devices: 31.2 us -> 29.9 us
    ppermute x4, waiting for transfers between devices: 1.66 us -> 9.66 us  [x_shift(): return lax.ppermute(value, ('x', 'core'), route)]
    ppermute x4, starting transfers between devices: 9.51 us -> 3.7 us  [x_shift(): return lax.ppermute(value, ('x', 'core'), route)]
    ppermute x1, waiting for transfers between devices: 0.01 us -> 5.26 us  [per_device(): mirrored = lax.ppermute(reverse_tracks, SEQ, mirror)]
    ppermute x1, waiting for transfers between devices: 5.34 us -> 0.45 us  [per_device(): away = lax.ppermute(away, SEQ, mirror)]
    ppermute x3, starting transfers between devices: 2.74 us -> 6.07 us  [y_shift(): return lax.ppermute(value, ('y_hi', 'y_lo', 'core'), route)]
    ppermute x9, starting transfers between devices: 4.86 us -> 6.43 us  [core_swap(): return lax.ppermute(value, 'core', [(0, 1), (1, 0)])]
    ppermute x1, waiting for transfers between devices: 1.19 us -> 0.01 us  [z_shift(): return lax.ppermute(value, ('z', 'core'), route)]
    ppermute x3, waiting for transfers between devices: 1.92 us -> 0.85 us  [y_shift(): return lax.ppermute(value, ('y_hi', 'y_lo', 'core'), route)]
  transfers between devices with their start and end apart: 21 -> 21, of which waited for: 6 -> 7; matrix products, arithmetic and copies ran while one was open for 1% -> 1% of each run, Pallas kernels for 41% -> 39%
where the time goes in v2:
time: 85.6 us; the launch traced here: 85.4 us
  Pallas kernels  34.3 us (40%)
  starting transfers between devices  29.9 us (35%)
  waiting for transfers between devices  17.5 us (20%)
  local copies, waits for them, and re-layouts  2.22 us (3%)
  other arithmetic  1.22 us (1%)
    ppermute x4, waiting for transfers between devices, x_shift(): return lax.ppermute(value, ('x', 'core'), route)  9.66 us
    pallas_call x2, Pallas kernels, finish(): pl.pallas_call(functools.partial(finish_kernel, flipped, len(sources)), o...  9.28 us
    pallas_call x2, Pallas kernels, partial_sum(): pl.pallas_call(functools.partial(partial_kernel, len(sources), prev is No...  9.28 us
    ppermute x9, starting transfers between devices, core_swap(): return lax.ppermute(value, 'core', [(0, 1), (1, 0)])  6.43 us
    ppermute x3, starting transfers between devices, y_shift(): return lax.ppermute(value, ('y_hi', 'y_lo', 'core'), route)  6.07 us
    pallas_call x1, Pallas kernels, prepare(): pl.pallas_call(prepare_kernel, out_shape=stripes(rows + EDGE) + stripes(k...  5.69 us
    ppermute x1, starting transfers between devices, z_shift(): return lax.ppermute(value, ('z', 'core'), route)  5.57 us
    pallas_call x1, Pallas kernels, whole(): pl.pallas_call(functools.partial(whole_kernel, SOURCES), out_shape=jax.Sh...  5.41 us
  transfers between devices with their start and end apart: 21, of which 7 were waited for; matrix products, arithmetic and copies ran while one was open for 1% of the time, Pallas kernels for 39%

profile of v2, /device:TPU:1, one launch (start us, length us, event | category | flops | bytes accessed | tf_op | source)
XLA Modules:
  0.0 85.4 jit_solution(3031768326428128869)
XLA Ops:
  0.0 3.2 %collective-permute-start.7 = (bf16[3,96,1536]{2,1,0:T(8,128)(2,1)}, bf16[3,96,1536]{2,1,0:T(8,128)(2,1)S(1)}, u32[]{:S(2)}, u32[]{:S(2)}) collective-permute-start(bf16[3,96,1536]{2,1,0:T(8,128)(2,1)} %bitcast.34), channel_id=1, source_target_pairs={{0,1},{1,0},{2,3},{3,2},{4,5},{5,4},{6,7},{7,6},{8,9},{9,8},{10,11... | collective-permute-start | bytes 2654216 | tf_op jit(solution)/shard_map/sibling/ppermute | solution.py:28
  3.2 1.0 %collective-permute-start.1 = (bf16[3,96,1536]{2,1,0:T(8,128)(2,1)}, bf16[3,96,1536]{2,1,0:T(8,128)(2,1)S(1)}, u32[]{:S(2)}, u32[]{:S(2)}) collective-permute-start(bf16[3,96,1536]{2,1,0:T(8,128)(2,1)} %bitcast.35), channel_id=1, source_target_pairs={{0,2},{1,131},{2,128},{3,1},{128,130},{129,3},{130,0},{131,129},{4... | collective-permute-start | bytes 2654216 | tf_op jit(solution)/shard_map/across/ppermute | solution.py:42
  4.2 2.5 %collective-permute-start = (bf16[3,96,1536]{2,1,0:T(8,128)(2,1)}, bf16[3,96,1536]{2,1,0:T(8,128)(2,1)S(1)}, u32[]{:S(2)}, u32[]{:S(2)}) collective-permute-start(bf16[3,96,1536]{2,1,0:T(8,128)(2,1)} %bitcast.36), channel_id=1, source_target_pairs={{0,4},{1,13},{4,8},{5,1},{8,12},{9,5},{12,0},{13,9},{2,6},{3,15},{... | collective-permute-start | bytes 2654216 | tf_op jit(solution)/shard_map/near/ppermute | solution.py:35
  6.7 0.8 fusion
  7.6 1.9 %collective-permute-start.2 = (bf16[2,1536]{1,0:T(2,128)(2,1)S(1)}, bf16[2,1536]{1,0:T(2,128)(2,1)S(1)}, u32[]{:S(2)}, u32[]{:S(2)}) collective-permute-start(bf16[2,1536]{1,0:T(2,128)(2,1)S(1)} %pad_maximum_fusion), channel_id=1, source_target_pairs={{0,1},{1,2},{2,3},{3,4},{4,5},{5,6},{6,7},{7,8},{8,9},{9,10},{10,1... | collective-permute-start | bytes 18440 | tf_op jit(solution)/shard_map/low/ppermute | solution.py:402
  9.5 2.4 %collective-permute-start.3 = (bf16[2,1536]{1,0:T(2,128)(2,1)S(1)}, bf16[2,1536]{1,0:T(2,128)(2,1)S(1)}, u32[]{:S(2)}, u32[]{:S(2)}) collective-permute-start(bf16[2,1536]{1,0:T(2,128)(2,1)S(1)} %pad_maximum_fusion.1), channel_id=1, source_target_pairs={{1,0},{2,1},{3,2},{4,3},{5,4},{6,5},{7,6},{8,7},{9,8},{10,9},{11,1... | collective-permute-start | bytes 18440 | tf_op jit(solution)/shard_map/high/ppermute | solution.py:404
  12.0 0.1 stack.137.place_ref
  12.1 0.0 copy-start.5
  12.1 1.3 %copy-done.5 = bf16[384,1536]{1,0:T(8,128)(2,1)S(1)} copy-done((bf16[384,1536]{1,0:T(8,128)(2,1)S(1)}, bf16[384,1536]{1,0:T(8,128)(2,1)}, u32[]{:S(2)}) %copy-start.5) | copy-done | bytes 1179672
  13.4 3.1 %order.1 = (bf16[1536,576]{1,0:T(8,128)(2,1)S(1)}, bf16[1536,384]{1,0:T(8,128)(2,1)S(1)}, bf16[1536,576]{1,0:T(8,128)(2,1)S(1)}, bf16[384,1536]{1,0:T(8,128)(2,1)S(1)}, f32[8,128]{1,0:T(8,128)S(1)}) custom-call(s32[32]{0:T(128)S(1)} %stack.137.place_ref, bf16[384,1536]{1,0:T(8,128)(2,1)S(1)} %copy-done.5), custom_call_target="tpu_custom_call" | custom-call | flops 14495514624 | bytes 4718592 | tf_op jit(solution)/shard_map/order/pallas_call | solution.py:147
  16.5 0.0 copy-start.1
  16.5 0.5 collective-permute-done.refs_0_
  17.0 0.2 fence.3
  17.2 0.8 collective-permute-start.6
  18.0 0.1 collective-permute-start.9
  18.1 3.0 %collective-permute-start.5 = (bf16[3,96,1536]{2,1,0:T(8,128)(2,1)S(1)}, bf16[3,96,1536]{2,1,0:T(8,128)(2,1)S(1)}, u32[]{:S(2)}, u32[]{:S(2)}) collective-permute-start(bf16[3,96,1536]{2,1,0:T(8,128)(2,1)S(1)} %get-tuple-element.44.refs_6_.refs_7_), channel_id=1, source_target_pairs={{0,2},{1,131},{2,128},{3,1},{128,130},{129,3},{130,0},{131,129},{4... | collective-permute-start | bytes 2654216 | tf_op jit(solution)/shard_map/near_over/ppermute | solution.py:42
  21.1 0.2 collective-permute-start.4
  21.3 0.6 halve.1
  21.9 0.3 collective-permute-start.8
  22.3 5.7 %prepare.1 = (bf16[400,576]{1,0:T(8,128)(2,1)S(1)}, bf16[400,384]{1,0:T(8,128)(2,1)S(1)}, bf16[400,576]{1,0:T(8,128)(2,1)S(1)}, bf16[272,576]{1,0:T(8,128)(2,1)S...) custom-call(bf16[384,1536]{1,0:T(8,128)(2,1)S(1)} %copy-done.1, ...), custom_call_target="tpu_custom_call" | custom-call | flops 1000 | bytes 1000 | tf_op jit(solution)/shard_map/prepare/pallas_call | solution.py:206
  28.0 5.4 %partial_sum.2 = (f32[384,1536]{1,0:T(8,128)S(1)}, f32[256,1536]{1,0:T(8,128)S(1)}, f32[8,128]{1,0:T(8,128)S(1)}) custom-call(bf16[400,576]{1,0:T(8,128)(2,1)S(1)} %get-tuple-element.46.refs_0_, bf16[272,576]{1,0:T(8,128)(2,1)S(1)} %get-tuple-element.47.refs_1_, bf16[3,96,1536]{2,1,0:T(8,128)(2,1)S(1)} %bitcast.37, ...), custom_call_target="tpu_custom_call" | custom-call | flops 3397386240 | bytes 5308416 | tf_op jit(solution)/shard_map/partial_sum/pallas_call | solution.py:255
  33.4 4.6 %collective-permute-done.8.refs_3_ = bf16[3,48,1536]{2,1,0:T(8,128)(2,1)S(1)} collective-permute-done((bf16[3,48,1536]{2,1,0:T(8,128)(2,1)S(1)}, bf16[3,48,1536]{2,1,0:T(8,128)(2,1)S(1)}, u32[]{:S(2)}, u32[]{:S(2)}) %collective-permute-start.8) | collective-permute-done | bytes 442400 | tf_op jit(solution)/shard_map/second/ppermute | solution.py:35
  38.0 0.4 fence.4
  38.4 1.0 %collective-permute-start.13 = (bf16[3,96,1536]{2,1,0:T(8,128)(2,1)S(1)}, bf16[3,96,1536]{2,1,0:T(8,128)(2,1)S(1)}, u32[]{:S(2)}, u32[]{:S(2)}) collective-permute-start(bf16[3,96,1536]{2,1,0:T(8,128)(2,1)S(1)} %get-tuple-element.54.refs_2_.refs_9_), channel_id=1, source_target_pairs={{0,1},{1,0},{2,3},{3,2},{4,5},{5,4},{6,7},{7,6},{8,9},{9,8},{10,11... | collective-permute-start | bytes 2654216 | tf_op jit(solution)/shard_map/near_over_b/ppermute | solution.py:28
  39.4 0.1 collective-permute-start.14
  39.5 5.6 %collective-permute-start.12 = (bf16[3,48,1536]{2,1,0:T(8,128)(2,1)S(1)}, bf16[3,48,1536]{2,1,0:T(8,128)(2,1)S(1)}, u32[]{:S(2)}, u32[]{:S(2)}) collective-permute-start(bf16[3,48,1536]{2,1,0:T(8,128)(2,1)S(1)} %get-tuple-element.49.source_ref.refs_0_.refs_13_), channel_id=1, source_target_pairs={{0,16},{1,113},{16,32},{17,1},{32,48},{33,17},{48,64},{49,33},{64,... | collective-permute-start | bytes 1327112 | tf_op jit(solution)/shard_map/second_z/ppermute | solution.py:49
  45.1 0.6 collective-permute-start.10
  45.7 2.1 %collective-permute-start.11 = (bf16[3,96,1536]{2,1,0:T(8,128)(2,1)S(1)}, bf16[3,96,1536]{2,1,0:T(8,128)(2,1)S(1)}, u32[]{:S(2)}, u32[]{:S(2)}) collective-permute-start(bf16[3,96,1536]{2,1,0:T(8,128)(2,1)S(1)} %get-tuple-element.51.refs_4_.refs_11_), channel_id=1, source_target_pairs={{0,2},{1,131},{2,128},{3,1},{128,130},{129,3},{130,0},{131,129},{4... | collective-permute-start | bytes 2654216 | tf_op jit(solution)/shard_map/distant_over/ppermute | solution.py:42
  47.8 3.9 %partial_sum.3 = (f32[384,1536]{1,0:T(8,128)S(1)}, f32[256,1536]{1,0:T(8,128)S(1)}, f32[8,128]{1,0:T(8,128)S(1)}) custom-call(bf16[400,384]{1,0:T(8,128)(2,1)S(1)} %get-tuple-element.52.refs_0_, bf16[272,384]{1,0:T(8,128)(2,1)S(1)} %get-tuple-element.53.refs_1_, ...), custom_call_target="tpu_custom_call", output_to_operand_aliasing={{0}: (6, {}), {1}: (7, {})} | custom-call | flops 2264924160 | bytes 3538944 | tf_op jit(solution)/shard_map/partial_sum/pallas_call | solution.py:255
  51.8 0.0 copy-start
  51.8 0.0 copy-start.3
  51.8 0.0 copy-start.4
  51.8 0.4 collective-permute-start.15
  52.2 0.2 collective-permute-start.16
  52.4 4.5 %collective-permute-done.10.refs_0_ = bf16[3,96,1536]{2,1,0:T(8,128)(2,1)S(1)} collective-permute-done((bf16[3,96,1536]{2,1,0:T(8,128)(2,1)S(1)}, bf16[3,96,1536]{2,1,0:T(8,128)(2,1)S(1)}, u32[]{:S(2)}, u32[]{:S(2)}) %collective-permute-start.10) | collective-permute-done | bytes 884768 | tf_op jit(solution)/shard_map/second_over/ppermute | solution.py:35
  57.0 0.8 collective-permute-done.11.refs_1_
  57.8 0.4 fence.5
  58.2 0.1 collective-permute-start.17
  58.3 0.5 collective-permute-start.18
  58.8 1.9 %collective-permute-start.20 = (bf16[144,1536]{1,0:T(8,128)(2,1)S(1)}, bf16[144,1536]{1,0:T(8,128)(2,1)S(1)}, u32[]{:S(2)}, u32[]{:S(2)}) collective-permute-start(bf16[144,1536]{1,0:T(8,128)(2,1)S(1)} %get-tuple-element.66), channel_id=1, source_target_pairs={{0,15},{1,14},{2,13},{3,12},{4,11},{5,10},{6,9},{7,8},{8,7},{9,6},... | collective-permute-start | bytes 1327112 | tf_op jit(solution)/shard_map/away/ppermute | solution.py:444
  60.7 1.2 %collective-permute-done.18.refs_7_.refs_20_ = bf16[3,96,1536]{2,1,0:T(8,128)(2,1)S(1)} collective-permute-done((bf16[3,96,1536]{2,1,0:T(8,128)(2,1)S(1)}, bf16[3,96,1536]{2,1,0:T(8,128)(2,1)S(1)}, u32[]{:S(2)}, u32[]{:S(2)}) %collective-permute-start.18) | collective-permute-done | bytes 884768 | tf_op jit(solution)/shard_map/distant_over_b/ppermute | solution.py:28
  62.0 3.8 %finish.3 = bf16[256,1024]{1,0:T(8,128)(2,1)S(1)} custom-call(bf16[272,576]{1,0:T(8,128)(2,1)S(1)} %get-tuple-element.64.x_ref, bf16[3,48,1536]{2,1,0:T(8,128)(2,1)S(1)} %get-tuple-element.49.source_ref.refs_0_.refs_13_, bf16[3,48,1536]{2,1,0:T(8,128)(2,1)S(1)} %get-tuple-element.59.refs_1_.refs_14_, ...), custom_call_target="tpu_custom_call" | custom-call | flops 2164260864 | bytes 8454144 | tf_op jit(solution)/shard_map/finish/pallas_call | solution.py:304
  65.8 1.8 %collective-permute-start.19 = (bf16[256,1024]{1,0:T(8,128)(2,1)S(1)}, bf16[256,1024]{1,0:T(8,128)(2,1)S(1)}, u32[]{:S(2)}, u32[]{:S(2)}) collective-permute-start(bf16[256,1024]{1,0:T(8,128)(2,1)S(1)} %finish.3), channel_id=1, source_target_pairs={{0,15},{1,14},{2,13},{3,12},{4,11},{5,10},{6,9},{7,8},{8,7},{9,6},... | collective-permute-start | bytes 1572872 | tf_op jit(solution)/shard_map/mirrored/ppermute | solution.py:453
  67.6 5.5 %finish.2.forward_ref = bf16[384,1024]{1,0:T(8,128)(2,1)S(1)} custom-call(bf16[400,576]{1,0:T(8,128)(2,1)S(1)} %get-tuple-element.43.x_ref, bf16[3,48,1536]{2,1,0:T(8,128)(2,1)S(1)} %get-tuple-element.49.source_ref.refs_0_.refs_13_, bf16[3,48,1536]{2,1,0:T(8,128)(2,1)S(1)} %get-tuple-element.59.refs_1_.refs_14_, ...), custom_call_target="tpu_custom_call" | custom-call | flops 3246391296 | bytes 8454144 | tf_op jit(solution)/shard_map/finish/pallas_call | solution.py:304
  73.1 0.4 collective-permute-done.20.away_ref
  73.6 5.4 %whole.1 = bf16[128,1024]{1,0:T(8,128)(2,1)S(1)} custom-call(bf16[384,1024]{1,0:T(8,128)(2,1)S(1)} %finish.2.forward_ref, bf16[144,1536]{1,0:T(8,128)(2,1)S(1)} %collective-permute-done.20.away_ref, bf16[1536,576]{1,0:T(8,128)(2,1)S(1)} %get-tuple-element.40.refs_0_, bf16[1536,384]{1,0:T(8,128)(2,1)S(1)} %get-tuple-element.41.refs_1_, ...), custom_call_target="tpu_custom_call" | custom-call | flops 2818572288 | bytes 14155776 | tf_op jit(solution)/shard_map/whole/pallas_call | solution.py:344
  79.0 5.3 %collective-permute-done.19 = bf16[256,1024]{1,0:T(8,128)(2,1)S(1)} collective-permute-done((bf16[256,1024]{1,0:T(8,128)(2,1)S(1)}, bf16[256,1024]{1,0:T(8,128)(2,1)S(1)}, u32[]{:S(2)}, u32[]{:S(2)}) %collective-permute-start.19) | collective-permute-done | bytes 524320 | tf_op jit(solution)/shard_map/mirrored/ppermute | solution.py:453
  84.2 1.2 %multiply_convert_fusion = bf16[384,1024]{1,0:T(8,128)(2,1)} fusion(bf16[384,1024]{1,0:T(8,128)(2,1)S(1)} %finish.2.forward_ref, bf16[128,1024]{1,0:T(8,128)(2,1)S(1)} %whole.1, bf16[256,1024]{1,0:T(8,128)(2,1)S(1)} %collective-permute-done.19), kind=kLoop, calls=%fused_computation | loop fusion | flops 3145728 | bytes 2359296 | tf_op jit(solution)/shard_map/convert_element_type | solution.py:458
  (24 shorter events, 0.2 us)
Async XLA Ops:
  0.0 21.3 %collective-permute-start.7 = (bf16[3,96,1536]{2,1,0:T(8,128)(2,1)}, bf16[3,96,1536]{2,1,0:T(8,128)(2,1)S(1)}, u32[]{:S(2)}, u32[]{:S(2)}) collective-permute-start(bf16[3,96,1536]{2,1,0:T(8,128)(2,1)} %bitcast.34), channel_id=1, source_target_pairs={{0,1},{1,0},{2,3},{3,2},{4,5},{5,4},{6,7},{7,6},{8,9},{9,8},{10,11... | collective-permute-start | bytes 2654216 | tf_op jit(solution)/shard_map/sibling/ppermute | solution.py:28
  3.2 13.3 %collective-permute-start.1 = (bf16[3,96,1536]{2,1,0:T(8,128)(2,1)}, bf16[3,96,1536]{2,1,0:T(8,128)(2,1)S(1)}, u32[]{:S(2)}, u32[]{:S(2)}) collective-permute-start(bf16[3,96,1536]{2,1,0:T(8,128)(2,1)} %bitcast.35), channel_id=1, source_target_pairs={{0,2},{1,131},{2,128},{3,1},{128,130},{129,3},{130,0},{131,129},{4... | collective-permute-start | bytes 2654216 | tf_op jit(solution)/shard_map/across/ppermute | solution.py:42
  4.2 12.8 %collective-permute-start = (bf16[3,96,1536]{2,1,0:T(8,128)(2,1)}, bf16[3,96,1536]{2,1,0:T(8,128)(2,1)S(1)}, u32[]{:S(2)}, u32[]{:S(2)}) collective-permute-start(bf16[3,96,1536]{2,1,0:T(8,128)(2,1)} %bitcast.36), channel_id=1, source_target_pairs={{0,4},{1,13},{4,8},{5,1},{8,12},{9,5},{12,0},{13,9},{2,6},{3,15},{... | collective-permute-start | bytes 2654216 | tf_op jit(solution)/shard_map/near/ppermute | solution.py:35
  7.6 8.9 %collective-permute-start.2 = (bf16[2,1536]{1,0:T(2,128)(2,1)S(1)}, bf16[2,1536]{1,0:T(2,128)(2,1)S(1)}, u32[]{:S(2)}, u32[]{:S(2)}) collective-permute-start(bf16[2,1536]{1,0:T(2,128)(2,1)S(1)} %pad_maximum_fusion), channel_id=1, source_target_pairs={{0,1},{1,2},{2,3},{3,4},{4,5},{5,6},{6,7},{7,8},{8,9},{9,10},{10,1... | collective-permute-start | bytes 18440 | tf_op jit(solution)/shard_map/low/ppermute | solution.py:402
  9.5 7.0 %collective-permute-start.3 = (bf16[2,1536]{1,0:T(2,128)(2,1)S(1)}, bf16[2,1536]{1,0:T(2,128)(2,1)S(1)}, u32[]{:S(2)}, u32[]{:S(2)}) collective-permute-start(bf16[2,1536]{1,0:T(2,128)(2,1)S(1)} %pad_maximum_fusion.1), channel_id=1, source_target_pairs={{1,0},{2,1},{3,2},{4,3},{5,4},{6,5},{7,6},{8,7},{9,8},{10,9},{11,1... | collective-permute-start | bytes 18440 | tf_op jit(solution)/shard_map/high/ppermute | solution.py:404
  12.1 1.3 %copy-start.5 = (bf16[384,1536]{1,0:T(8,128)(2,1)S(1)}, bf16[384,1536]{1,0:T(8,128)(2,1)}, u32[]{:S(2)}) copy-start(bf16[384,1536]{1,0:T(8,128)(2,1)} %reverse_ref.1) | copy-start | bytes 3538948
  16.5 5.8 %copy-start.1 = (bf16[384,1536]{1,0:T(8,128)(2,1)S(1)}, bf16[384,1536]{1,0:T(8,128)(2,1)}, u32[]{:S(2)}) copy-start(bf16[384,1536]{1,0:T(8,128)(2,1)} %forward_ref.1) | copy-start | bytes 3538948
  17.2 10.7 %collective-permute-start.6 = (bf16[3,96,1536]{2,1,0:T(8,128)(2,1)S(1)}, bf16[3,96,1536]{2,1,0:T(8,128)(2,1)S(1)}, u32[]{:S(2)}, u32[]{:S(2)}) collective-permute-start(bf16[3,96,1536]{2,1,0:T(8,128)(2,1)S(1)} %get-tuple-element.45.refs_4_.refs_5_), channel_id=1, source_target_pairs={{0,1},{1,0},{2,3},{3,2},{4,5},{5,4},{6,7},{7,6},{8,9},{9,8},{10,11... | collective-permute-start | bytes 2654216 | tf_op jit(solution)/shard_map/across_b/ppermute | solution.py:28
  18.0 9.9 %collective-permute-start.9 = (bf16[3,96,1536]{2,1,0:T(8,128)(2,1)S(1)}, bf16[3,96,1536]{2,1,0:T(8,128)(2,1)S(1)}, u32[]{:S(2)}, u32[]{:S(2)}) collective-permute-start(bf16[3,96,1536]{2,1,0:T(8,128)(2,1)S(1)} %get-tuple-element.44.refs_6_.refs_7_), channel_id=1, source_target_pairs={{0,1},{1,0},{2,3},{3,2},{4,5},{5,4},{6,7},{7,6},{8,9},{9,8},{10,11... | collective-permute-start | bytes 2654216 | tf_op jit(solution)/shard_map/near_b/ppermute | solution.py:28
  18.1 19.9 %collective-permute-start.5 = (bf16[3,96,1536]{2,1,0:T(8,128)(2,1)S(1)}, bf16[3,96,1536]{2,1,0:T(8,128)(2,1)S(1)}, u32[]{:S(2)}, u32[]{:S(2)}) collective-permute-start(bf16[3,96,1536]{2,1,0:T(8,128)(2,1)S(1)} %get-tuple-element.44.refs_6_.refs_7_), channel_id=1, source_target_pairs={{0,2},{1,131},{2,128},{3,1},{128,130},{129,3},{130,0},{131,129},{4... | collective-permute-start | bytes 2654216 | tf_op jit(solution)/shard_map/near_over/ppermute | solution.py:42
  21.1 16.9 %collective-permute-start.4 = (bf16[3,96,1536]{2,1,0:T(8,128)(2,1)S(1)}, bf16[3,96,1536]{2,1,0:T(8,128)(2,1)S(1)}, u32[]{:S(2)}, u32[]{:S(2)}) collective-permute-start(bf16[3,96,1536]{2,1,0:T(8,128)(2,1)S(1)} %get-tuple-element.44.refs_6_.refs_7_), channel_id=1, source_target_pairs={{0,4},{1,13},{4,8},{5,1},{8,12},{9,5},{12,0},{13,9},{2,6},{3,15},{... | collective-permute-start | bytes 2654216 | tf_op jit(solution)/shard_map/distant/ppermute | solution.py:35
  21.9 16.1 %collective-permute-start.8 = (bf16[3,48,1536]{2,1,0:T(8,128)(2,1)S(1)}, bf16[3,48,1536]{2,1,0:T(8,128)(2,1)S(1)}, u32[]{:S(2)}, u32[]{:S(2)}) collective-permute-start(bf16[3,48,1536]{2,1,0:T(8,128)(2,1)S(1)} %halve.1), channel_id=1, source_target_pairs={{0,4},{1,13},{4,8},{5,1},{8,12},{9,5},{12,0},{13,9},{2,6},{3,15},{... | collective-permute-start | bytes 1327112 | tf_op jit(solution)/shard_map/second/ppermute | solution.py:35
  22.3 5.7 %copy-start.2 = (bf16[1,3,96,1536]{3,2,1,0:T(8,128)(2,1)S(1)}, bf16[1,3,96,1536]{3,2,1,0:T(8,128)(2,1)}, u32[]{:S(2)}) copy-start(bf16[1,3,96,1536]{3,2,1,0:T(8,128)(2,1)} %param.8) | copy-start | bytes 2654212
  38.4 9.5 %collective-permute-start.13 = (bf16[3,96,1536]{2,1,0:T(8,128)(2,1)S(1)}, bf16[3,96,1536]{2,1,0:T(8,128)(2,1)S(1)}, u32[]{:S(2)}, u32[]{:S(2)}) collective-permute-start(bf16[3,96,1536]{2,1,0:T(8,128)(2,1)S(1)} %get-tuple-element.54.refs_2_.refs_9_), channel_id=1, source_target_pairs={{0,1},{1,0},{2,3},{3,2},{4,5},{5,4},{6,7},{7,6},{8,9},{9,8},{10,11... | collective-permute-start | bytes 2654216 | tf_op jit(solution)/shard_map/near_over_b/ppermute | solution.py:28
  39.4 8.4 %collective-permute-start.14 = (bf16[3,96,1536]{2,1,0:T(8,128)(2,1)S(1)}, bf16[3,96,1536]{2,1,0:T(8,128)(2,1)S(1)}, u32[]{:S(2)}, u32[]{:S(2)}) collective-permute-start(bf16[3,96,1536]{2,1,0:T(8,128)(2,1)S(1)} %get-tuple-element.51.refs_4_.refs_11_), channel_id=1, source_target_pairs={{0,1},{1,0},{2,3},{3,2},{4,5},{5,4},{6,7},{7,6},{8,9},{9,8},{10,11... | collective-permute-start | bytes 2654216 | tf_op jit(solution)/shard_map/distant_b/ppermute | solution.py:28
  39.5 12.3 %collective-permute-start.12 = (bf16[3,48,1536]{2,1,0:T(8,128)(2,1)S(1)}, bf16[3,48,1536]{2,1,0:T(8,128)(2,1)S(1)}, u32[]{:S(2)}, u32[]{:S(2)}) collective-permute-start(bf16[3,48,1536]{2,1,0:T(8,128)(2,1)S(1)} %get-tuple-element.49.source_ref.refs_0_.refs_13_), channel_id=1, source_target_pairs={{0,16},{1,113},{16,32},{17,1},{32,48},{33,17},{48,64},{49,33},{64,... | collective-permute-start | bytes 1327112 | tf_op jit(solution)/shard_map/second_z/ppermute | solution.py:49
  45.1 11.9 %collective-permute-start.10 = (bf16[3,96,1536]{2,1,0:T(8,128)(2,1)S(1)}, bf16[3,96,1536]{2,1,0:T(8,128)(2,1)S(1)}, u32[]{:S(2)}, u32[]{:S(2)}) collective-permute-start(bf16[3,96,1536]{2,1,0:T(8,128)(2,1)S(1)} %get-tuple-element.50.refs_6_), channel_id=1, source_target_pairs={{0,4},{1,13},{4,8},{5,1},{8,12},{9,5},{12,0},{13,9},{2,6},{3,15},{... | collective-permute-start | bytes 2654216 | tf_op jit(solution)/shard_map/second_over/ppermute | solution.py:35
  45.7 12.1 %collective-permute-start.11 = (bf16[3,96,1536]{2,1,0:T(8,128)(2,1)S(1)}, bf16[3,96,1536]{2,1,0:T(8,128)(2,1)S(1)}, u32[]{:S(2)}, u32[]{:S(2)}) collective-permute-start(bf16[3,96,1536]{2,1,0:T(8,128)(2,1)S(1)} %get-tuple-element.51.refs_4_.refs_11_), channel_id=1, source_target_pairs={{0,2},{1,131},{2,128},{3,1},{128,130},{129,3},{130,0},{131,129},{4... | collective-permute-start | bytes 2654216 | tf_op jit(solution)/shard_map/distant_over/ppermute | solution.py:42
  51.8 10.2 %copy-start = (bf16[1536,1024]{1,0:T(8,128)(2,1)S(1)}, bf16[1536,1024]{1,0:T(8,128)(2,1)}, u32[]{:S(2)}) copy-start(bf16[1536,1024]{1,0:T(8,128)(2,1)} %refs_22_.1) | copy-start | bytes 9437188
  51.8 10.2 %copy-start.3 = (f32[1,1536]{1,0:T(1,128)S(1)}, f32[1,1536]{1,0:T(1,128)}, u32[]{:S(2)}) copy-start(f32[1,1536]{1,0:T(1,128)} %refs_21_.1) | copy-start | bytes 18436
  51.8 10.1 %copy-start.4 = (f32[1024]{0:T(1024)S(1)}, f32[1024]{0:T(1024)}, u32[]{:S(2)}) copy-start(f32[1024]{0:T(1024)} %param.11) | copy-start | bytes 12292
  51.8 6.0 %collective-permute-start.15 = (bf16[3,48,1536]{2,1,0:T(8,128)(2,1)S(1)}, bf16[3,48,1536]{2,1,0:T(8,128)(2,1)S(1)}, u32[]{:S(2)}, u32[]{:S(2)}) collective-permute-start(bf16[3,48,1536]{2,1,0:T(8,128)(2,1)S(1)} %after.2), channel_id=1, source_target_pairs={{0,1},{1,0},{2,3},{3,2},{4,5},{5,4},{6,7},{7,6},{8,9},{9,8},{10,11... | collective-permute-start | bytes 1327112 | tf_op jit(solution)/shard_map/second_z_b/ppermute | solution.py:28
  52.2 5.6 %collective-permute-start.16 = (bf16[3,48,1536]{2,1,0:T(8,128)(2,1)S(1)}, bf16[3,48,1536]{2,1,0:T(8,128)(2,1)S(1)}, u32[]{:S(2)}, u32[]{:S(2)}) collective-permute-start(bf16[3,48,1536]{2,1,0:T(8,128)(2,1)S(1)} %after.3), channel_id=1, source_target_pairs={{0,1},{1,0},{2,3},{3,2},{4,5},{5,4},{6,7},{7,6},{8,9},{9,8},{10,11... | collective-permute-start | bytes 1327112 | tf_op jit(solution)/shard_map/second_b/ppermute | solution.py:28
  58.2 2.5 %collective-permute-start.17 = (bf16[3,96,1536]{2,1,0:T(8,128)(2,1)S(1)}, bf16[3,96,1536]{2,1,0:T(8,128)(2,1)S(1)}, u32[]{:S(2)}, u32[]{:S(2)}) collective-permute-start(bf16[3,96,1536]{2,1,0:T(8,128)(2,1)S(1)} %get-tuple-element.61.refs_4_.refs_17_), channel_id=1, source_target_pairs={{0,1},{1,0},{2,3},{3,2},{4,5},{5,4},{6,7},{7,6},{8,9},{9,8},{10,11... | collective-permute-start | bytes 2654216 | tf_op jit(solution)/shard_map/second_over_b/ppermute | solution.py:28
  58.3 3.7 %collective-permute-start.18 = (bf16[3,96,1536]{2,1,0:T(8,128)(2,1)S(1)}, bf16[3,96,1536]{2,1,0:T(8,128)(2,1)S(1)}, u32[]{:S(2)}, u32[]{:S(2)}) collective-permute-start(bf16[3,96,1536]{2,1,0:T(8,128)(2,1)S(1)} %get-tuple-element.62.refs_6_.refs_19_), channel_id=1, source_target_pairs={{0,1},{1,0},{2,3},{3,2},{4,5},{5,4},{6,7},{7,6},{8,9},{9,8},{10,11... | collective-permute-start | bytes 2654216 | tf_op jit(solution)/shard_map/distant_over_b/ppermute | solution.py:28
  58.8 14.8 %collective-permute-start.20 = (bf16[144,1536]{1,0:T(8,128)(2,1)S(1)}, bf16[144,1536]{1,0:T(8,128)(2,1)S(1)}, u32[]{:S(2)}, u32[]{:S(2)}) collective-permute-start(bf16[144,1536]{1,0:T(8,128)(2,1)S(1)} %get-tuple-element.66), channel_id=1, source_target_pairs={{0,15},{1,14},{2,13},{3,12},{4,11},{5,10},{6,9},{7,8},{8,7},{9,6},... | collective-permute-start | bytes 1327112 | tf_op jit(solution)/shard_map/away/ppermute | solution.py:444
  65.8 18.4 %collective-permute-start.19 = (bf16[256,1024]{1,0:T(8,128)(2,1)S(1)}, bf16[256,1024]{1,0:T(8,128)(2,1)S(1)}, u32[]{:S(2)}, u32[]{:S(2)}) collective-permute-start(bf16[256,1024]{1,0:T(8,128)(2,1)S(1)} %finish.3), channel_id=1, source_target_pairs={{0,15},{1,14},{2,13},{3,12},{4,11},{5,10},{6,9},{7,8},{8,7},{9,6},... | collective-permute-start | bytes 1572872 | tf_op jit(solution)/shard_map/mirrored/ppermute | solution.py:453

commit v3 on v1

--- a/solution.py
+++ b/solution.py
@@ -18,8 +18,8 @@
 SOURCES = (6, 4, 8)
 PIECES = 32
 FIRST_HALF = 20
-ROWS = 128
-AWAY = 128
+ROWS = 96
+AWAY = 96
 TOKEN = jax.ShapeDtypeStruct((8, 128), jnp.float32)
 INV_SQRT2 = 0.7071067811865476
 

time: 80.9 us -> 80.7 us (level)
  waiting for transfers between devices: 11.6 us -> 10.2 us
  Pallas kernels: 34.2 us -> 35.4 us
    ppermute x1, waiting for transfers between devices: 5.34 us -> 1.57 us  [per_device(): away = lax.ppermute(away, SEQ, mirror)]
    ppermute x1, waiting for transfers between devices: 0.01 us -> 2.84 us  [per_device(): mirrored = lax.ppermute(reverse_tracks, SEQ, mirror)]
    pallas_call x2, Pallas kernels: 9.25 us -> 10.5 us  [finish(): pl.pallas_call(functools.partial(finish_kernel, flipped, len(sources)), o...]
  transfers between devices with their start and end apart: 21 -> 21, of which waited for: 6 -> 7; matrix products, arithmetic and copies ran while one was open for 1% -> 1% of each run, Pallas kernels for 41% -> 43%
where the time goes in v3:
time: 80.7 us; the launch traced here: 80.4 us
  Pallas kernels  35.4 us (44%)
  starting transfers between devices  31.2 us (39%)
  waiting for transfers between devices  10.2 us (13%)
  local copies, waits for them, and re-layouts  2.22 us (3%)
  other arithmetic  1.21 us (1%)
    pallas_call x2, Pallas kernels, finish(): pl.pallas_call(functools.partial(finish_kernel, flipped, len(sources)), o...  10.5 us
    pallas_call x2, Pallas kernels, partial_sum(): pl.pallas_call(functools.partial(partial_kernel, len(sources), prev is No...  9.68 us
    ppermute x4, starting transfers between devices, x_shift(): return lax.ppermute(value, ('x', 'core'), route)  9.51 us
    pallas_call x1, Pallas kernels, prepare(): pl.pallas_call(prepare_kernel, out_shape=stripes(rows + EDGE) + stripes(k...  5.73 us
    ppermute x1, starting transfers between devices, z_shift(): return lax.ppermute(value, ('z', 'core'), route)  5.52 us
    ppermute x9, starting transfers between devices, core_swap(): return lax.ppermute(value, 'core', [(0, 1), (1, 0)])  4.86 us
    pallas_call x1, Pallas kernels, whole(): pl.pallas_call(functools.partial(whole_kernel, SOURCES), out_shape=jax.Sh...  4.83 us
    pallas_call x1, Pallas kernels, order(): pl.pallas_call(order_kernel, out_shape=[jax.ShapeDtypeStruct((width, coun...  3.07 us
  transfers between devices with their start and end apart: 21, of which 7 were waited for; matrix products, arithmetic and copies ran while one was open for 1% of the time, Pallas kernels for 43%

profile of v3, /device:TPU:1, one launch (start us, length us, event | category | flops | bytes accessed | tf_op | source)
XLA Modules:
  0.0 80.4 jit_solution(11224625412390210512)
XLA Ops:
  0.0 3.3 %collective-permute-start = (bf16[3,96,1536]{2,1,0:T(8,128)(2,1)}, bf16[3,96,1536]{2,1,0:T(8,128)(2,1)S(1)}, u32[]{:S(2)}, u32[]{:S(2)}) collective-permute-start(bf16[3,96,1536]{2,1,0:T(8,128)(2,1)} %bitcast.34), channel_id=1, source_target_pairs={{0,4},{1,13},{4,8},{5,1},{8,12},{9,5},{12,0},{13,9},{2,6},{3,15},{... | collective-permute-start | bytes 2654216 | tf_op jit(solution)/shard_map/near/ppermute | solution.py:35
  3.3 2.7 %collective-permute-start.1 = (bf16[3,96,1536]{2,1,0:T(8,128)(2,1)}, bf16[3,96,1536]{2,1,0:T(8,128)(2,1)S(1)}, u32[]{:S(2)}, u32[]{:S(2)}) collective-permute-start(bf16[3,96,1536]{2,1,0:T(8,128)(2,1)} %bitcast.35), channel_id=1, source_target_pairs={{0,2},{1,131},{2,128},{3,1},{128,130},{129,3},{130,0},{131,129},{4... | collective-permute-start | bytes 2654216 | tf_op jit(solution)/shard_map/across/ppermute | solution.py:42
  6.0 0.8 %fusion = (bf16[1,1536]{1,0:T(2,128)(2,1)S(1)}, bf16[1,1536]{1,0:T(2,128)(2,1)S(1)}, bf16[1,1536]{1,0:T(2,128)(2,1)S(1)}, bf16[1,1536]{1,0:T(2,128)(2,1)S(1)}) fusion(bf16[384,1536]{1,0:T(8,128)(2,1)} %forward_ref.1, bf16[384,1536]{1,0:T(8,128)(2,1)} %reverse_ref.1), kind=kLoop, calls=%fused_computation.3 | loop fusion | bytes 24576 | tf_op jit(solution)/shard_map/high/slice | solution.py:404
  6.9 1.9 %collective-permute-start.2 = (bf16[2,1536]{1,0:T(2,128)(2,1)S(1)}, bf16[2,1536]{1,0:T(2,128)(2,1)S(1)}, u32[]{:S(2)}, u32[]{:S(2)}) collective-permute-start(bf16[2,1536]{1,0:T(2,128)(2,1)S(1)} %pad_maximum_fusion), channel_id=1, source_target_pairs={{0,1},{1,2},{2,3},{3,4},{4,5},{5,6},{6,7},{7,8},{8,9},{9,10},{10,1... | collective-permute-start | bytes 18440 | tf_op jit(solution)/shard_map/low/ppermute | solution.py:402
  8.8 2.4 %collective-permute-start.3 = (bf16[2,1536]{1,0:T(2,128)(2,1)S(1)}, bf16[2,1536]{1,0:T(2,128)(2,1)S(1)}, u32[]{:S(2)}, u32[]{:S(2)}) collective-permute-start(bf16[2,1536]{1,0:T(2,128)(2,1)S(1)} %pad_maximum_fusion.1), channel_id=1, source_target_pairs={{1,0},{2,1},{3,2},{4,3},{5,4},{6,5},{7,6},{8,7},{9,8},{10,9},{11,1... | collective-permute-start | bytes 18440 | tf_op jit(solution)/shard_map/high/ppermute | solution.py:404
  11.3 0.1 stack.137.place_ref
  11.4 0.0 copy-start.5
  11.5 1.3 %copy-done.5 = bf16[384,1536]{1,0:T(8,128)(2,1)S(1)} copy-done((bf16[384,1536]{1,0:T(8,128)(2,1)S(1)}, bf16[384,1536]{1,0:T(8,128)(2,1)}, u32[]{:S(2)}) %copy-start.5) | copy-done | bytes 1179672
  12.7 3.1 %order.1 = (bf16[1536,576]{1,0:T(8,128)(2,1)S(1)}, bf16[1536,384]{1,0:T(8,128)(2,1)S(1)}, bf16[1536,576]{1,0:T(8,128)(2,1)S(1)}, bf16[384,1536]{1,0:T(8,128)(2,1)S(1)}, f32[8,128]{1,0:T(8,128)S(1)}) custom-call(s32[32]{0:T(128)S(1)} %stack.137.place_ref, bf16[384,1536]{1,0:T(8,128)(2,1)S(1)} %copy-done.5), custom_call_target="tpu_custom_call" | custom-call | flops 14495514624 | bytes 4718592 | tf_op jit(solution)/shard_map/order/pallas_call | solution.py:147
  15.8 0.0 copy-start.1
  15.8 0.0 collective-permute-done.3.refs_3_
  15.8 0.0 collective-permute-done.refs_0_
  15.8 0.5 collective-permute-done.1.refs_1_
  16.3 0.2 fence.3
  16.6 1.4 %collective-permute-start.6 = (bf16[3,96,1536]{2,1,0:T(8,128)(2,1)S(1)}, bf16[3,96,1536]{2,1,0:T(8,128)(2,1)S(1)}, u32[]{:S(2)}, u32[]{:S(2)}) collective-permute-start(bf16[3,96,1536]{2,1,0:T(8,128)(2,1)S(1)} %get-tuple-element.45.refs_4_.refs_5_), channel_id=1, source_target_pairs={{0,1},{1,0},{2,3},{3,2},{4,5},{5,4},{6,7},{7,6},{8,9},{9,8},{10,11... | collective-permute-start | bytes 2654216 | tf_op jit(solution)/shard_map/across_b/ppermute | solution.py:28
  18.0 0.1 collective-permute-start.9
  18.1 3.0 %collective-permute-start.4 = (bf16[3,96,1536]{2,1,0:T(8,128)(2,1)S(1)}, bf16[3,96,1536]{2,1,0:T(8,128)(2,1)S(1)}, u32[]{:S(2)}, u32[]{:S(2)}) collective-permute-start(bf16[3,96,1536]{2,1,0:T(8,128)(2,1)S(1)} %get-tuple-element.44.refs_6_.refs_7_), channel_id=1, source_target_pairs={{0,4},{1,13},{4,8},{5,1},{8,12},{9,5},{12,0},{13,9},{2,6},{3,15},{... | collective-permute-start | bytes 2654216 | tf_op jit(solution)/shard_map/distant/ppermute | solution.py:35
  21.1 0.0 collective-permute-done.7.shard_ref.refs_3_.refs_4_
  21.1 0.6 halve.1
  21.7 1.4 %collective-permute-start.8 = (bf16[3,48,1536]{2,1,0:T(8,128)(2,1)S(1)}, bf16[3,48,1536]{2,1,0:T(8,128)(2,1)S(1)}, u32[]{:S(2)}, u32[]{:S(2)}) collective-permute-start(bf16[3,48,1536]{2,1,0:T(8,128)(2,1)S(1)} %halve.1), channel_id=1, source_target_pairs={{0,4},{1,13},{4,8},{5,1},{8,12},{9,5},{12,0},{13,9},{2,6},{3,15},{... | collective-permute-start | bytes 1327112 | tf_op jit(solution)/shard_map/second/ppermute | solution.py:35
  23.1 5.7 %prepare.1 = (bf16[400,576]{1,0:T(8,128)(2,1)S(1)}, bf16[400,384]{1,0:T(8,128)(2,1)S(1)}, bf16[400,576]{1,0:T(8,128)(2,1)S(1)}, bf16[304,576]{1,0:T(8,128)(2,1)S...) custom-call(bf16[384,1536]{1,0:T(8,128)(2,1)S(1)} %copy-done.1, ...), custom_call_target="tpu_custom_call" | custom-call | flops 1000 | bytes 1000 | tf_op jit(solution)/shard_map/prepare/pallas_call | solution.py:206
  28.9 5.6 %partial_sum.2 = (f32[384,1536]{1,0:T(8,128)S(1)}, f32[288,1536]{1,0:T(8,128)S(1)}, f32[8,128]{1,0:T(8,128)S(1)}) custom-call(bf16[400,576]{1,0:T(8,128)(2,1)S(1)} %get-tuple-element.46.refs_0_, bf16[304,576]{1,0:T(8,128)(2,1)S(1)} %get-tuple-element.47.refs_1_, bf16[3,96,1536]{2,1,0:T(8,128)(2,1)S(1)} %bitcast.37, ...), custom_call_target="tpu_custom_call" | custom-call | flops 3567255552 | bytes 5308416 | tf_op jit(solution)/shard_map/partial_sum/pallas_call | solution.py:255
  34.5 1.3 %collective-permute-done.8.refs_3_ = bf16[3,48,1536]{2,1,0:T(8,128)(2,1)S(1)} collective-permute-done((bf16[3,48,1536]{2,1,0:T(8,128)(2,1)S(1)}, bf16[3,48,1536]{2,1,0:T(8,128)(2,1)S(1)}, u32[]{:S(2)}, u32[]{:S(2)}) %collective-permute-start.8) | collective-permute-done | bytes 442400 | tf_op jit(solution)/shard_map/second/ppermute | solution.py:35
  35.8 0.4 fence.4
  36.2 1.8 %collective-permute-start.13 = (bf16[3,96,1536]{2,1,0:T(8,128)(2,1)S(1)}, bf16[3,96,1536]{2,1,0:T(8,128)(2,1)S(1)}, u32[]{:S(2)}, u32[]{:S(2)}) collective-permute-start(bf16[3,96,1536]{2,1,0:T(8,128)(2,1)S(1)} %get-tuple-element.54.refs_2_.refs_9_), channel_id=1, source_target_pairs={{0,1},{1,0},{2,3},{3,2},{4,5},{5,4},{6,7},{7,6},{8,9},{9,8},{10,11... | collective-permute-start | bytes 2654216 | tf_op jit(solution)/shard_map/near_over_b/ppermute | solution.py:28
  38.0 0.1 collective-permute-start.14
  38.1 1.8 %collective-permute-start.10 = (bf16[3,96,1536]{2,1,0:T(8,128)(2,1)S(1)}, bf16[3,96,1536]{2,1,0:T(8,128)(2,1)S(1)}, u32[]{:S(2)}, u32[]{:S(2)}) collective-permute-start(bf16[3,96,1536]{2,1,0:T(8,128)(2,1)S(1)} %get-tuple-element.50.refs_6_), channel_id=1, source_target_pairs={{0,4},{1,13},{4,8},{5,1},{8,12},{9,5},{12,0},{13,9},{2,6},{3,15},{... | collective-permute-start | bytes 2654216 | tf_op jit(solution)/shard_map/second_over/ppermute | solution.py:35
  39.9 5.5 %collective-permute-start.12 = (bf16[3,48,1536]{2,1,0:T(8,128)(2,1)S(1)}, bf16[3,48,1536]{2,1,0:T(8,128)(2,1)S(1)}, u32[]{:S(2)}, u32[]{:S(2)}) collective-permute-start(bf16[3,48,1536]{2,1,0:T(8,128)(2,1)S(1)} %get-tuple-element.49.source_ref.refs_0_.refs_13_), channel_id=1, source_target_pairs={{0,16},{1,113},{16,32},{17,1},{32,48},{33,17},{48,64},{49,33},{64,... | collective-permute-start | bytes 1327112 | tf_op jit(solution)/shard_map/second_z/ppermute | solution.py:49
  45.4 4.0 %partial_sum.3 = (f32[384,1536]{1,0:T(8,128)S(1)}, f32[288,1536]{1,0:T(8,128)S(1)}, f32[8,128]{1,0:T(8,128)S(1)}) custom-call(bf16[400,384]{1,0:T(8,128)(2,1)S(1)} %get-tuple-element.52.refs_0_, bf16[304,384]{1,0:T(8,128)(2,1)S(1)} %get-tuple-element.53.refs_1_, ...), custom_call_target="tpu_custom_call", output_to_operand_aliasing={{0}: (6, {}), {1}: (7, {})} | custom-call | flops 2378170368 | bytes 3538944 | tf_op jit(solution)/shard_map/partial_sum/pallas_call | solution.py:255
  49.5 0.0 copy-start
  49.5 0.0 copy-start.3
  49.5 0.0 copy-start.4
  49.5 0.1 collective-permute-start.15
  49.6 1.0 %collective-permute-done.12.refs_2_ = bf16[3,48,1536]{2,1,0:T(8,128)(2,1)S(1)} collective-permute-done((bf16[3,48,1536]{2,1,0:T(8,128)(2,1)S(1)}, bf16[3,48,1536]{2,1,0:T(8,128)(2,1)S(1)}, u32[]{:S(2)}, u32[]{:S(2)}) %collective-permute-start.12) | collective-permute-done | bytes 442400 | tf_op jit(solution)/shard_map/second_z/ppermute | solution.py:49
  50.7 1.4 %collective-permute-done.11.refs_1_ = bf16[3,96,1536]{2,1,0:T(8,128)(2,1)S(1)} collective-permute-done((bf16[3,96,1536]{2,1,0:T(8,128)(2,1)S(1)}, bf16[3,96,1536]{2,1,0:T(8,128)(2,1)S(1)}, u32[]{:S(2)}, u32[]{:S(2)}) %collective-permute-start.11) | collective-permute-done | bytes 884768 | tf_op jit(solution)/shard_map/distant_over/ppermute | solution.py:42
  52.1 0.3 fence.5
  52.4 0.8 collective-permute-start.17
  53.2 0.1 collective-permute-start.18
  53.3 0.4 collective-permute-start.16
  53.7 1.9 %collective-permute-start.20 = (bf16[112,1536]{1,0:T(8,128)(2,1)S(1)}, bf16[112,1536]{1,0:T(8,128)(2,1)S(1)}, u32[]{:S(2)}, u32[]{:S(2)}) collective-permute-start(bf16[112,1536]{1,0:T(8,128)(2,1)S(1)} %get-tuple-element.66), channel_id=1, source_target_pairs={{0,15},{1,14},{2,13},{3,12},{4,11},{5,10},{6,9},{7,8},{8,7},{9,6},... | collective-permute-start | bytes 1032200 | tf_op jit(solution)/shard_map/away/ppermute | solution.py:442
  55.7 1.5 %collective-permute-done.16.refs_3_.refs_16_ = bf16[3,48,1536]{2,1,0:T(8,128)(2,1)S(1)} collective-permute-done((bf16[3,48,1536]{2,1,0:T(8,128)(2,1)S(1)}, bf16[3,48,1536]{2,1,0:T(8,128)(2,1)S(1)}, u32[]{:S(2)}, u32[]{:S(2)}) %collective-permute-start.16) | collective-permute-done | bytes 442400 | tf_op jit(solution)/shard_map/second_z_b/ppermute | solution.py:28
  57.2 4.5 %finish.3 = bf16[288,1024]{1,0:T(8,128)(2,1)S(1)} custom-call(bf16[304,576]{1,0:T(8,128)(2,1)S(1)} %get-tuple-element.64.x_ref, bf16[3,48,1536]{2,1,0:T(8,128)(2,1)S(1)} %get-tuple-element.49.source_ref.refs_0_.refs_13_, bf16[3,48,1536]{2,1,0:T(8,128)(2,1)S(1)} %get-tuple-element.59.refs_1_.refs_14_, ...), custom_call_target="tpu_custom_call" | custom-call | flops 2434793472 | bytes 8454144 | tf_op jit(solution)/shard_map/finish/pallas_call | solution.py:304
  61.8 2.3 %collective-permute-start.19 = (bf16[288,1024]{1,0:T(8,128)(2,1)S(1)}, bf16[288,1024]{1,0:T(8,128)(2,1)S(1)}, u32[]{:S(2)}, u32[]{:S(2)}) collective-permute-start(bf16[288,1024]{1,0:T(8,128)(2,1)S(1)} %finish.3), channel_id=1, source_target_pairs={{0,15},{1,14},{2,13},{3,12},{4,11},{5,10},{6,9},{7,8},{8,7},{9,6},... | collective-permute-start | bytes 1769480 | tf_op jit(solution)/shard_map/mirrored/ppermute | solution.py:453
  64.0 1.6 %collective-permute-done.20.away_ref = bf16[112,1536]{1,0:T(8,128)(2,1)S(1)} collective-permute-done((bf16[112,1536]{1,0:T(8,128)(2,1)S(1)}, bf16[112,1536]{1,0:T(8,128)(2,1)S(1)}, u32[]{:S(2)}, u32[]{:S(2)}) %collective-permute-start.20) | collective-permute-done | bytes 344096 | tf_op jit(solution)/shard_map/away/ppermute | solution.py:442
  65.6 4.8 %whole.1 = bf16[96,1024]{1,0:T(8,128)(2,1)S(1)} custom-call(bf16[112,1536]{1,0:T(8,128)(2,1)S(1)} %collective-permute-done.20.away_ref, bf16[1536,576]{1,0:T(8,128)(2,1)S(1)} %get-tuple-element.40.refs_0_, bf16[1536,384]{1,0:T(8,128)(2,1)S(1)} %get-tuple-element.41.refs_1_, bf16[1536,576]{1,0:T(8,128)(2,1)S(1)} %get-tuple-element.42.refs_2_, ...), custom_call_target="tpu_custom_call" | custom-call | flops 2113929216 | bytes 14155776 | tf_op jit(solution)/shard_map/whole/pallas_call | solution.py:344
  70.4 6.0 %finish.2 = bf16[384,1024]{1,0:T(8,128)(2,1)S(1)} custom-call(bf16[400,576]{1,0:T(8,128)(2,1)S(1)} %get-tuple-element.43.x_ref, bf16[3,48,1536]{2,1,0:T(8,128)(2,1)S(1)} %get-tuple-element.49.source_ref.refs_0_.refs_13_, bf16[3,48,1536]{2,1,0:T(8,128)(2,1)S(1)} %get-tuple-element.59.refs_1_.refs_14_, ...), custom_call_target="tpu_custom_call" | custom-call | flops 3246391296 | bytes 8454144 | tf_op jit(solution)/shard_map/finish/pallas_call | solution.py:304
  76.4 2.8 %collective-permute-done.19 = bf16[288,1024]{1,0:T(8,128)(2,1)S(1)} collective-permute-done((bf16[288,1024]{1,0:T(8,128)(2,1)S(1)}, bf16[288,1024]{1,0:T(8,128)(2,1)S(1)}, u32[]{:S(2)}, u32[]{:S(2)}) %collective-permute-start.19) | collective-permute-done | bytes 589856 | tf_op jit(solution)/shard_map/mirrored/ppermute | solution.py:453
  79.3 1.2 %multiply_convert_fusion = bf16[384,1024]{1,0:T(8,128)(2,1)} fusion(bf16[384,1024]{1,0:T(8,128)(2,1)S(1)} %finish.2, bf16[96,1024]{1,0:T(8,128)(2,1)S(1)} %whole.1, bf16[288,1024]{1,0:T(8,128)(2,1)S(1)} %collective-permute-done.19), kind=kLoop, calls=%fused_computation | loop fusion | flops 3145728 | bytes 2359296 | tf_op jit(solution)/shard_map/convert_element_type | solution.py:458
  (23 shorter events, 0.1 us)
Async XLA Ops:
  0.0 15.8 %collective-permute-start = (bf16[3,96,1536]{2,1,0:T(8,128)(2,1)}, bf16[3,96,1536]{2,1,0:T(8,128)(2,1)S(1)}, u32[]{:S(2)}, u32[]{:S(2)}) collective-permute-start(bf16[3,96,1536]{2,1,0:T(8,128)(2,1)} %bitcast.34), channel_id=1, source_target_pairs={{0,4},{1,13},{4,8},{5,1},{8,12},{9,5},{12,0},{13,9},{2,6},{3,15},{... | collective-permute-start | bytes 2654216 | tf_op jit(solution)/shard_map/near/ppermute | solution.py:35
  3.3 13.0 %collective-permute-start.1 = (bf16[3,96,1536]{2,1,0:T(8,128)(2,1)}, bf16[3,96,1536]{2,1,0:T(8,128)(2,1)S(1)}, u32[]{:S(2)}, u32[]{:S(2)}) collective-permute-start(bf16[3,96,1536]{2,1,0:T(8,128)(2,1)} %bitcast.35), channel_id=1, source_target_pairs={{0,2},{1,131},{2,128},{3,1},{128,130},{129,3},{130,0},{131,129},{4... | collective-permute-start | bytes 2654216 | tf_op jit(solution)/shard_map/across/ppermute | solution.py:42
  6.0 15.0 %collective-permute-start.7 = (bf16[3,96,1536]{2,1,0:T(8,128)(2,1)}, bf16[3,96,1536]{2,1,0:T(8,128)(2,1)S(1)}, u32[]{:S(2)}, u32[]{:S(2)}) collective-permute-start(bf16[3,96,1536]{2,1,0:T(8,128)(2,1)} %bitcast.36), channel_id=1, source_target_pairs={{0,1},{1,0},{2,3},{3,2},{4,5},{5,4},{6,7},{7,6},{8,9},{9,8},{10,11... | collective-permute-start | bytes 2654216 | tf_op jit(solution)/shard_map/sibling/ppermute | solution.py:28
  6.9 8.9 %collective-permute-start.2 = (bf16[2,1536]{1,0:T(2,128)(2,1)S(1)}, bf16[2,1536]{1,0:T(2,128)(2,1)S(1)}, u32[]{:S(2)}, u32[]{:S(2)}) collective-permute-start(bf16[2,1536]{1,0:T(2,128)(2,1)S(1)} %pad_maximum_fusion), channel_id=1, source_target_pairs={{0,1},{1,2},{2,3},{3,4},{4,5},{5,6},{6,7},{7,8},{8,9},{9,10},{10,1... | collective-permute-start | bytes 18440 | tf_op jit(solution)/shard_map/low/ppermute | solution.py:402
  8.8 7.0 %collective-permute-start.3 = (bf16[2,1536]{1,0:T(2,128)(2,1)S(1)}, bf16[2,1536]{1,0:T(2,128)(2,1)S(1)}, u32[]{:S(2)}, u32[]{:S(2)}) collective-permute-start(bf16[2,1536]{1,0:T(2,128)(2,1)S(1)} %pad_maximum_fusion.1), channel_id=1, source_target_pairs={{1,0},{2,1},{3,2},{4,3},{5,4},{6,5},{7,6},{8,7},{9,8},{10,9},{11,1... | collective-permute-start | bytes 18440 | tf_op jit(solution)/shard_map/high/ppermute | solution.py:404
  11.4 1.3 %copy-start.5 = (bf16[384,1536]{1,0:T(8,128)(2,1)S(1)}, bf16[384,1536]{1,0:T(8,128)(2,1)}, u32[]{:S(2)}) copy-start(bf16[384,1536]{1,0:T(8,128)(2,1)} %reverse_ref.1) | copy-start | bytes 3538948
  15.8 7.3 %copy-start.1 = (bf16[384,1536]{1,0:T(8,128)(2,1)S(1)}, bf16[384,1536]{1,0:T(8,128)(2,1)}, u32[]{:S(2)}) copy-start(bf16[384,1536]{1,0:T(8,128)(2,1)} %forward_ref.1) | copy-start | bytes 3538948
  16.6 12.3 %collective-permute-start.6 = (bf16[3,96,1536]{2,1,0:T(8,128)(2,1)S(1)}, bf16[3,96,1536]{2,1,0:T(8,128)(2,1)S(1)}, u32[]{:S(2)}, u32[]{:S(2)}) collective-permute-start(bf16[3,96,1536]{2,1,0:T(8,128)(2,1)S(1)} %get-tuple-element.45.refs_4_.refs_5_), channel_id=1, source_target_pairs={{0,1},{1,0},{2,3},{3,2},{4,5},{5,4},{6,7},{7,6},{8,9},{9,8},{10,11... | collective-permute-start | bytes 2654216 | tf_op jit(solution)/shard_map/across_b/ppermute | solution.py:28
  18.0 10.8 %collective-permute-start.9 = (bf16[3,96,1536]{2,1,0:T(8,128)(2,1)S(1)}, bf16[3,96,1536]{2,1,0:T(8,128)(2,1)S(1)}, u32[]{:S(2)}, u32[]{:S(2)}) collective-permute-start(bf16[3,96,1536]{2,1,0:T(8,128)(2,1)S(1)} %get-tuple-element.44.refs_6_.refs_7_), channel_id=1, source_target_pairs={{0,1},{1,0},{2,3},{3,2},{4,5},{5,4},{6,7},{7,6},{8,9},{9,8},{10,11... | collective-permute-start | bytes 2654216 | tf_op jit(solution)/shard_map/near_b/ppermute | solution.py:28
  18.1 17.7 %collective-permute-start.4 = (bf16[3,96,1536]{2,1,0:T(8,128)(2,1)S(1)}, bf16[3,96,1536]{2,1,0:T(8,128)(2,1)S(1)}, u32[]{:S(2)}, u32[]{:S(2)}) collective-permute-start(bf16[3,96,1536]{2,1,0:T(8,128)(2,1)S(1)} %get-tuple-element.44.refs_6_.refs_7_), channel_id=1, source_target_pairs={{0,4},{1,13},{4,8},{5,1},{8,12},{9,5},{12,0},{13,9},{2,6},{3,15},{... | collective-permute-start | bytes 2654216 | tf_op jit(solution)/shard_map/distant/ppermute | solution.py:35
  21.1 14.7 %collective-permute-start.5 = (bf16[3,96,1536]{2,1,0:T(8,128)(2,1)S(1)}, bf16[3,96,1536]{2,1,0:T(8,128)(2,1)S(1)}, u32[]{:S(2)}, u32[]{:S(2)}) collective-permute-start(bf16[3,96,1536]{2,1,0:T(8,128)(2,1)S(1)} %get-tuple-element.44.refs_6_.refs_7_), channel_id=1, source_target_pairs={{0,2},{1,131},{2,128},{3,1},{128,130},{129,3},{130,0},{131,129},{4... | collective-permute-start | bytes 2654216 | tf_op jit(solution)/shard_map/near_over/ppermute | solution.py:42
  21.7 14.1 %collective-permute-start.8 = (bf16[3,48,1536]{2,1,0:T(8,128)(2,1)S(1)}, bf16[3,48,1536]{2,1,0:T(8,128)(2,1)S(1)}, u32[]{:S(2)}, u32[]{:S(2)}) collective-permute-start(bf16[3,48,1536]{2,1,0:T(8,128)(2,1)S(1)} %halve.1), channel_id=1, source_target_pairs={{0,4},{1,13},{4,8},{5,1},{8,12},{9,5},{12,0},{13,9},{2,6},{3,15},{... | collective-permute-start | bytes 1327112 | tf_op jit(solution)/shard_map/second/ppermute | solution.py:35
  23.1 5.7 %copy-start.2 = (bf16[1,3,96,1536]{3,2,1,0:T(8,128)(2,1)S(1)}, bf16[1,3,96,1536]{3,2,1,0:T(8,128)(2,1)}, u32[]{:S(2)}) copy-start(bf16[1,3,96,1536]{3,2,1,0:T(8,128)(2,1)} %param.8) | copy-start | bytes 2654212
  36.2 9.2 %collective-permute-start.13 = (bf16[3,96,1536]{2,1,0:T(8,128)(2,1)S(1)}, bf16[3,96,1536]{2,1,0:T(8,128)(2,1)S(1)}, u32[]{:S(2)}, u32[]{:S(2)}) collective-permute-start(bf16[3,96,1536]{2,1,0:T(8,128)(2,1)S(1)} %get-tuple-element.54.refs_2_.refs_9_), channel_id=1, source_target_pairs={{0,1},{1,0},{2,3},{3,2},{4,5},{5,4},{6,7},{7,6},{8,9},{9,8},{10,11... | collective-permute-start | bytes 2654216 | tf_op jit(solution)/shard_map/near_over_b/ppermute | solution.py:28
  38.0 7.4 %collective-permute-start.14 = (bf16[3,96,1536]{2,1,0:T(8,128)(2,1)S(1)}, bf16[3,96,1536]{2,1,0:T(8,128)(2,1)S(1)}, u32[]{:S(2)}, u32[]{:S(2)}) collective-permute-start(bf16[3,96,1536]{2,1,0:T(8,128)(2,1)S(1)} %get-tuple-element.51.refs_4_.refs_11_), channel_id=1, source_target_pairs={{0,1},{1,0},{2,3},{3,2},{4,5},{5,4},{6,7},{7,6},{8,9},{9,8},{10,11... | collective-permute-start | bytes 2654216 | tf_op jit(solution)/shard_map/distant_b/ppermute | solution.py:28
  38.1 12.6 %collective-permute-start.10 = (bf16[3,96,1536]{2,1,0:T(8,128)(2,1)S(1)}, bf16[3,96,1536]{2,1,0:T(8,128)(2,1)S(1)}, u32[]{:S(2)}, u32[]{:S(2)}) collective-permute-start(bf16[3,96,1536]{2,1,0:T(8,128)(2,1)S(1)} %get-tuple-element.50.refs_6_), channel_id=1, source_target_pairs={{0,4},{1,13},{4,8},{5,1},{8,12},{9,5},{12,0},{13,9},{2,6},{3,15},{... | collective-permute-start | bytes 2654216 | tf_op jit(solution)/shard_map/second_over/ppermute | solution.py:35
  39.9 12.2 %collective-permute-start.11 = (bf16[3,96,1536]{2,1,0:T(8,128)(2,1)S(1)}, bf16[3,96,1536]{2,1,0:T(8,128)(2,1)S(1)}, u32[]{:S(2)}, u32[]{:S(2)}) collective-permute-start(bf16[3,96,1536]{2,1,0:T(8,128)(2,1)S(1)} %get-tuple-element.51.refs_4_.refs_11_), channel_id=1, source_target_pairs={{0,2},{1,131},{2,128},{3,1},{128,130},{129,3},{130,0},{131,129},{4... | collective-permute-start | bytes 2654216 | tf_op jit(solution)/shard_map/distant_over/ppermute | solution.py:42
  39.9 10.8 %collective-permute-start.12 = (bf16[3,48,1536]{2,1,0:T(8,128)(2,1)S(1)}, bf16[3,48,1536]{2,1,0:T(8,128)(2,1)S(1)}, u32[]{:S(2)}, u32[]{:S(2)}) collective-permute-start(bf16[3,48,1536]{2,1,0:T(8,128)(2,1)S(1)} %get-tuple-element.49.source_ref.refs_0_.refs_13_), channel_id=1, source_target_pairs={{0,16},{1,113},{16,32},{17,1},{32,48},{33,17},{48,64},{49,33},{64,... | collective-permute-start | bytes 1327112 | tf_op jit(solution)/shard_map/second_z/ppermute | solution.py:49
  49.5 7.7 %copy-start = (bf16[1536,1024]{1,0:T(8,128)(2,1)S(1)}, bf16[1536,1024]{1,0:T(8,128)(2,1)}, u32[]{:S(2)}) copy-start(bf16[1536,1024]{1,0:T(8,128)(2,1)} %refs_22_.1) | copy-start | bytes 9437188
  49.5 7.7 %copy-start.3 = (f32[1,1536]{1,0:T(1,128)S(1)}, f32[1,1536]{1,0:T(1,128)}, u32[]{:S(2)}) copy-start(f32[1,1536]{1,0:T(1,128)} %refs_21_.1) | copy-start | bytes 18436
  49.5 7.7 %copy-start.4 = (f32[1024]{0:T(1024)S(1)}, f32[1024]{0:T(1024)}, u32[]{:S(2)}) copy-start(f32[1024]{0:T(1024)} %param.11) | copy-start | bytes 12292
  49.5 2.5 %collective-permute-start.15 = (bf16[3,48,1536]{2,1,0:T(8,128)(2,1)S(1)}, bf16[3,48,1536]{2,1,0:T(8,128)(2,1)S(1)}, u32[]{:S(2)}, u32[]{:S(2)}) collective-permute-start(bf16[3,48,1536]{2,1,0:T(8,128)(2,1)S(1)} %after.1), channel_id=1, source_target_pairs={{0,1},{1,0},{2,3},{3,2},{4,5},{5,4},{6,7},{7,6},{8,9},{9,8},{10,11... | collective-permute-start | bytes 1327112 | tf_op jit(solution)/shard_map/second_b/ppermute | solution.py:28
  52.4 4.7 %collective-permute-start.17 = (bf16[3,96,1536]{2,1,0:T(8,128)(2,1)S(1)}, bf16[3,96,1536]{2,1,0:T(8,128)(2,1)S(1)}, u32[]{:S(2)}, u32[]{:S(2)}) collective-permute-start(bf16[3,96,1536]{2,1,0:T(8,128)(2,1)S(1)} %get-tuple-element.61.refs_4_.refs_17_), channel_id=1, source_target_pairs={{0,1},{1,0},{2,3},{3,2},{4,5},{5,4},{6,7},{7,6},{8,9},{9,8},{10,11... | collective-permute-start | bytes 2654216 | tf_op jit(solution)/shard_map/second_over_b/ppermute | solution.py:28
  53.2 4.0 %collective-permute-start.18 = (bf16[3,96,1536]{2,1,0:T(8,128)(2,1)S(1)}, bf16[3,96,1536]{2,1,0:T(8,128)(2,1)S(1)}, u32[]{:S(2)}, u32[]{:S(2)}) collective-permute-start(bf16[3,96,1536]{2,1,0:T(8,128)(2,1)S(1)} %get-tuple-element.62.refs_6_.refs_19_), channel_id=1, source_target_pairs={{0,1},{1,0},{2,3},{3,2},{4,5},{5,4},{6,7},{7,6},{8,9},{9,8},{10,11... | collective-permute-start | bytes 2654216 | tf_op jit(solution)/shard_map/distant_over_b/ppermute | solution.py:28
  53.3 3.9 %collective-permute-start.16 = (bf16[3,48,1536]{2,1,0:T(8,128)(2,1)S(1)}, bf16[3,48,1536]{2,1,0:T(8,128)(2,1)S(1)}, u32[]{:S(2)}, u32[]{:S(2)}) collective-permute-start(bf16[3,48,1536]{2,1,0:T(8,128)(2,1)S(1)} %get-tuple-element.60.refs_2_.refs_15_), channel_id=1, source_target_pairs={{0,1},{1,0},{2,3},{3,2},{4,5},{5,4},{6,7},{7,6},{8,9},{9,8},{10,11... | collective-permute-start | bytes 1327112 | tf_op jit(solution)/shard_map/second_z_b/ppermute | solution.py:28
  53.7 11.9 %collective-permute-start.20 = (bf16[112,1536]{1,0:T(8,128)(2,1)S(1)}, bf16[112,1536]{1,0:T(8,128)(2,1)S(1)}, u32[]{:S(2)}, u32[]{:S(2)}) collective-permute-start(bf16[112,1536]{1,0:T(8,128)(2,1)S(1)} %get-tuple-element.66), channel_id=1, source_target_pairs={{0,15},{1,14},{2,13},{3,12},{4,11},{5,10},{6,9},{7,8},{8,7},{9,6},... | collective-permute-start | bytes 1032200 | tf_op jit(solution)/shard_map/away/ppermute | solution.py:442
  61.8 17.5 %collective-permute-start.19 = (bf16[288,1024]{1,0:T(8,128)(2,1)S(1)}, bf16[288,1024]{1,0:T(8,128)(2,1)S(1)}, u32[]{:S(2)}, u32[]{:S(2)}) collective-permute-start(bf16[288,1024]{1,0:T(8,128)(2,1)S(1)} %finish.3), channel_id=1, source_target_pairs={{0,15},{1,14},{2,13},{3,12},{4,11},{5,10},{6,9},{7,8},{8,7},{9,6},... | collective-permute-start | bytes 1769480 | tf_op jit(solution)/shard_map/mirrored/ppermute | solution.py:453
